TPU v7x, 512 devices: a whole 4x4x16 slice. The times are simulated.
512 devices in a mesh: site: 32 (over z_hi, y, x), mode: 16 (over z_lo, core).
Axes of the slice: x: 4, y: 4, z: 16 (z_hi: 2, z_lo: 8; z = z_hi * 8 + z_lo), core: 2. Of those that a mesh axis runs over, the one named last changes fastest.
Arguments:
- eigvecs: bfloat16 [64, 2, 4, 3, 4, 864, 128], P('mode', None, None, None, None, 'site'), may hold values from -1.59375 to 1.59375
- eigenvalues: float32 [64], P('mode'), may hold values from 0.5 to 4
- block_map: int32 [864], P('site'), may hold values from 0 to 863, each once
- momenta: int32 [27, 3], replicated, may hold values from -2 to 2
Outputs:
- loop_field: float32 [2, 16, 4, 864, 128], P(None, 'mode', None, 'site')
- loop_momentum: float32 [2, 16, 4, 27], replicated
Inputs may be any that keep to these rules, and one draw needn't show every extreme that they name: block_map names every spatial block once.
All inputs are finite; a program needn't handle non-finite values.
Results may differ from a plain program's by a relative error of at most 0.0003.
Values sent between devices are 32-bit elements; how exact they have to be, the bound alone decides.
A program may use at most 64 MiB of HBM per device.

v0:
```python
import math

import jax
import jax.numpy as jnp
import numpy as np
from jax import lax
from jax.sharding import PartitionSpec as P

L = 48


def gamma_table():
    unit = 1j
    first = np.array([[0, 0, 0, unit], [0, 0, unit, 0], [0, -unit, 0, 0], [-unit, 0, 0, 0]])
    second = np.array([[0, 0, 0, -1], [0, 0, 1, 0], [0, 1, 0, 0], [-1, 0, 0, 0]], dtype=complex)
    third = np.array([[0, 0, unit, 0], [0, 0, 0, -unit], [-unit, 0, 0, 0], [0, unit, 0, 0]])
    fourth = np.array([[0, 0, 1, 0], [0, 0, 0, 1], [1, 0, 0, 0], [0, 1, 0, 0]], dtype=complex)
    basis = [first, second, third, fourth]
    fifth = first @ second @ third @ fourth
    table = np.zeros((32, 32))
    for number in range(16):
        matrix = np.eye(4, dtype=complex)
        for bit in range(4):
            if number >> bit & 1:
                matrix = matrix @ basis[bit]
        matrix = matrix @ fifth
        flat_real = matrix.real.reshape(16)
        flat_imag = matrix.imag.reshape(16)
        table[number, :16] = flat_real
        table[number, 16:] = -flat_imag
        table[16 + number, :16] = flat_imag
        table[16 + number, 16:] = flat_real
    return table


def phase_tables(blocks, momenta, length):
    nby = length // 4
    nbz = length // 8
    inside = jnp.arange(128, dtype=jnp.int32)
    coord_x = 4 * (blocks // (nby * nbz))[:, None] + (inside // 32)[None, :]
    coord_y = 4 * (blocks // nbz % nby)[:, None] + (inside // 8 % 4)[None, :]
    coord_z = 8 * (blocks % nbz)[:, None] + (inside % 8)[None, :]
    coord_x = coord_x.reshape(-1)
    coord_y = coord_y.reshape(-1)
    coord_z = coord_z.reshape(-1)
    products = (
        coord_x[:, None] * momenta[None, :, 0]
        + coord_y[:, None] * momenta[None, :, 1]
        + coord_z[:, None] * momenta[None, :, 2]
    )
    wrapped = jnp.mod(products, length)
    angle = wrapped.astype(jnp.float32) * jnp.float32(2.0 * math.pi / length)
    return (jnp.cos(angle), jnp.sin(angle))


def project(field, cosine, sine, length):
    hp = lax.Precision.HIGHEST
    real_part = field[0]
    imag_part = field[1]
    out_real = jnp.einsum("gtx,xk->gtk", real_part, cosine, precision=hp) + jnp.einsum(
        "gtx,xk->gtk", imag_part, sine, precision=hp
    )
    out_imag = jnp.einsum("gtx,xk->gtk", imag_part, cosine, precision=hp) - jnp.einsum(
        "gtx,xk->gtk", real_part, sine, precision=hp
    )
    return jnp.stack([out_real, out_imag]) * jnp.float32(length ** (-1.5))


def shards(eigvecs, eigenvalues, block_map, momenta):
    hp = lax.Precision.HIGHEST
    local_modes = eigvecs.shape[0]
    slices = eigvecs.shape[4]
    slots = eigvecs.shape[5]
    count = slices * slots * 128
    weights = 1.0 / eigenvalues
    values = eigvecs.reshape(local_modes, 2, 4, 3, count)
    f32 = jnp.float32
    same = jnp.zeros((local_modes, 16, count), f32)
    cross = jnp.zeros((local_modes, 16, count), f32)
    for colour in range(3):
        real_col = values[:, 0, :, colour, :].astype(f32)
        imag_col = values[:, 1, :, colour, :].astype(f32)
        same = same + (
            real_col[:, :, None, :] * real_col[:, None, :, :]
            + imag_col[:, :, None, :] * imag_col[:, None, :, :]
        ).reshape(local_modes, 16, count)
        cross = cross + (
            real_col[:, :, None, :] * imag_col[:, None, :, :]
            - imag_col[:, :, None, :] * real_col[:, None, :, :]
        ).reshape(local_modes, 16, count)
    dens_real = jnp.sum(weights[:, None, None] * same, axis=0).reshape(4, 4, count)
    dens_imag = jnp.sum(weights[:, None, None] * cross, axis=0).reshape(4, 4, count)
    flat = jnp.concatenate([dens_real.reshape(16, count), dens_imag.reshape(16, count)], axis=0)
    table = jnp.asarray(gamma_table(), jnp.float32)
    partial_field = jnp.einsum("nk,kx->nx", table, flat, precision=hp).reshape(
        2, 16, slices, slots, 128
    )
    per_device = 16 // lax.axis_size("mode")
    offset = lax.axis_index("mode") * per_device
    summed = lax.psum(partial_field, "mode")
    share = lax.dynamic_slice_in_dim(summed, offset, per_device, 1)
    cosine, sine = phase_tables(block_map, momenta, L)
    own = project(share.reshape(2, per_device, slices, slots * 128), cosine, sine, L)
    padded = jnp.zeros((2, 16, slices, own.shape[3]), jnp.float32)
    padded = lax.dynamic_update_slice_in_dim(padded, own, offset, 1)
    loop_momentum = lax.psum(padded, ("site", "mode"))
    return (share, loop_momentum)


def solution(mesh):
    placed = (P("mode", None, None, None, None, "site", None), P("mode"), P("site"), P())
    return jax.shard_map(
        shards,
        mesh=mesh,
        in_specs=placed,
        out_specs=(P(None, "mode", None, "site", None), P()),
        check_vma=False,
    )
```

profile of v0, /device:TPU:1, one launch (start us, length us, event | category | flops | bytes accessed | tf_op | source)
XLA Modules:
  0.0 361.4 jit_solution(13188768697965813462)
XLA Ops:
  7.2 0.0 all-reduce.2.cloned.1.call-start
  7.2 2.7 copy.12
  9.9 2.7 reshape.271
  12.6 0.0 copy-start.4
  12.6 2.1 fusion.10
  14.7 0.0 copy-done.4
  14.7 8.7 %multiply_reduce_fusion = (f32[4,4,13824]{2,1,0:T(4,128)S(1)}, f32[4,4,13824]{2,1,0:T(4,128)S(1)}) fusion(f32[4,4,13824]{2,1,0:T(4,128)S(1)} %get-tuple-element.11, f32[4,4,13824]{2,1,0:T(4,128)S(1)} %get-tuple-element.12, f32[4,4,13824]{2,1,0:T(4,128)S(1)} %get-tuple-element.13, f32[4,4,13824]{2,1,0:T(4,128)S(1)} %get-tuple-element.14, ...), kind=kLoop, calls=%fused_computation.2 | loop fusion | flops 22560768 | bytes 7077904 | tf_op jit(solution)/shard_map/reduce_sum | solution.py:92
  23.4 0.0 copy-start
  23.4 0.0 copy-start.1
  23.4 0.3 reduce_sum.23
  23.8 0.3 reduce_sum.25
  24.1 0.1 copy-done
  24.1 1.5 fusion.47
  25.7 0.0 copy-done.1
  25.7 1.5 fusion
  27.2 0.0 copy-start.3
  27.2 0.0 copy-start.2
  27.2 1.7 reshape.272
  28.9 0.0 all-reduce.2.cloned.1.call-update
  28.9 0.0 copy-done.3
  29.0 0.0 copy-done.2
  29.0 0.1 add_bitcast_fusion
  29.1 0.1 add_bitcast_fusion.1
  29.1 0.1 add_bitcast_fusion.2
  29.2 209.0 %all-reduce.2.cloned.1.call-done = f32[2,16,4,27,128]{4,3,2,1,0:T(8,128)} async-done(((f32[2,16,4,27,128]{4,3,2,1,0:T(8,128)}), f32[2,16,4,27,128]{4,3,2,1,0:T(8,128)}) %all-reduce.2.cloned.1.call-update) | async-done | bytes 1769488 | tf_op jit(solution)/shard_map/psum | solution.py:100
  238.2 0.9 dynamic-slice_bitcast_fusion.1
  239.0 2.2 fusion.18
  241.3 2.2 fusion.16
  243.5 2.3 fusion.2
  245.8 2.2 fusion.1
  248.1 104.9 %psum.15 = f32[2,16,4,27]{3,2,1,0:T(4,128)} all-reduce(f32[2,16,4,27]{3,2,1,0:T(4,128)S(1)} %fusion.30), channel_id=1, replica_groups=mesh['site'=32,'mode'=16] {'site','mode'}, use_global_device_ids=true, to_apply=%region_3.4 | all-reduce | flops 3456 | bytes 27648 | tf_op jit(solution)/shard_map/psum | solution.py:106
  352.9 0.9 constant_dynamic-slice_fusion
  353.9 0.7 copy.13
  (7 shorter events, 0.1 us)
Async XLA Ops:
  7.2 231.0 %all-reduce.2.cloned.1.call-start = ((), (), s32[]{:S(2)}) async-start(), calls=%async_computation | async-start | bytes 4194304 | tf_op jit(solution)/shard_map/psum | solution.py:100
  12.6 2.1 copy-start.4
  23.4 0.7 copy-start
  23.4 2.2 copy-start.1
  27.2 1.7 copy-start.3
  27.2 1.8 copy-start.2
Sparse Core Ops, SparseCore 0:
  29.0 209.0 all-reduce.1
where the time goes:
time: 362 us; the launch traced here: 361 us
  waiting for transfers between devices  209 us (58%)
  blocking collectives  105 us (29%)
  between operations  14.2 us (4%)
  matrix products  12 us (3%)
  other arithmetic  11.1 us (3%)
  local copies, waits for them, and re-layouts  10.2 us (3%)
    psum x1, waiting for transfers between devices, shards(): summed = lax.psum(partial_field, 'mode')  209 us
    psum x1, blocking collectives, shards(): loop_momentum = lax.psum(padded, ('site', 'mode'))  105 us
    reduce_sum x1, other arithmetic, shards(): jnp.sum(weights[:, None, None] * cross, axis=0).reshape(4, 4, count)  8.7 us
  transfers between devices with their start and end apart: 1, of which 1 were waited for; matrix products, arithmetic and copies ran while one was open for 0% of the time, Pallas kernels for 0%

commit v1 on v0

--- a/solution.py
+++ b/solution.py
@@ -4,7 +4,11 @@
 import jax.numpy as jnp
 import numpy as np
 from jax import lax
+from jax.experimental import pallas as pl
+from jax.experimental.pallas import tpu as pltpu
 from jax.sharding import PartitionSpec as P
+
+MESH = pl.DeviceIdType.MESH
 
 L = 48
 
@@ -66,6 +70,47 @@
     return jnp.stack([out_real, out_imag]) * jnp.float32(length ** (-1.5))
 
 
+def along_z(site, mode, step):
+    z = site // 16 * 8 + mode // 2
+    to = lax.rem(z + step + 16, 16)
+    return (to // 8 * 16 + site % 16, to % 8 * 2 + mode % 2)
+
+
+def relay(x_ref, o_ref, got, token, send, recv):
+    site, mode = lax.axis_index("site"), lax.axis_index("mode")
+    near = pltpu.get_barrier_semaphore()
+    for step in (1, -1):
+        pl.semaphore_signal(near, inc=1, device_id=along_z(site, mode, step), device_id_type=MESH)
+    pl.semaphore_wait(near, 2)
+    for slot, step in enumerate((1, -1)):
+        pl.semaphore_signal(token.at[slot], inc=1, device_id=along_z(site, mode, step), device_id_type=MESH)
+    for slot in range(2):
+        pl.semaphore_wait(token.at[slot], 1)
+    copy = pltpu.make_async_remote_copy(
+        src_ref=x_ref, dst_ref=got, send_sem=send, recv_sem=recv,
+        device_id=along_z(site, mode, 2), device_id_type=MESH,
+    )
+    copy.start()
+    copy.wait()
+    o_ref[...] = got[...]
+
+
+def shift(x):
+    return pl.pallas_call(
+        relay,
+        out_shape=jax.ShapeDtypeStruct((8, 128), jnp.float32),
+        in_specs=[pl.BlockSpec(memory_space=pltpu.VMEM)],
+        out_specs=pl.BlockSpec(memory_space=pltpu.VMEM),
+        scratch_shapes=[
+            pltpu.VMEM((8, 128), jnp.float32),
+            pltpu.SemaphoreType.REGULAR((2,)),
+            pltpu.SemaphoreType.DMA,
+            pltpu.SemaphoreType.DMA,
+        ],
+        compiler_params=pltpu.CompilerParams(collective_id=0, has_side_effects=True),
+    )(x)
+
+
 def shards(eigvecs, eigenvalues, block_map, momenta):
     hp = lax.Precision.HIGHEST
     local_modes = eigvecs.shape[0]
@@ -103,6 +148,9 @@
     own = project(share.reshape(2, per_device, slices, slots * 128), cosine, sine, L)
     padded = jnp.zeros((2, 16, slices, own.shape[3]), jnp.float32)
     padded = lax.dynamic_update_slice_in_dim(padded, own, offset, 1)
+    flat_own = jnp.zeros((8, 128), jnp.float32) + momenta[0, 0].astype(jnp.float32)
+    moved = shift(flat_own)
+    padded = jnp.where(moved[0, 0] == flat_own[0, 0], padded, 0.0)
     loop_momentum = lax.psum(padded, ("site", "mode"))
     return (share, loop_momentum)
 

time: 362 us -> 362 us (level)
  waiting for transfers between devices: 209 us -> 190 us
  Pallas kernels: 0 us -> 14.9 us
    psum x1, waiting for transfers between devices: 209 us -> 190 us  [shards(): summed = lax.psum(partial_field, 'mode')]
    pallas_call x0 -> x1, Pallas kernels: none -> 14.9 us  [shift(): pl.pallas_call(relay, out_shape=jax.ShapeDtypeStruct((8, 128), jnp.float3...]
  transfers between devices with their start and end apart: 1 -> 1, of which waited for: 1 -> 1; matrix products, arithmetic and copies ran while one was open for 0% -> 1% of each run, Pallas kernels for 0% -> 4%
where the time goes in v1:
time: 362 us; the launch traced here: 361 us
  waiting for transfers between devices  190 us (52%)
  blocking collectives  105 us (29%)
  between operations  15.5 us (4%)
  Pallas kernels  14.9 us (4%)
  local copies, waits for them, and re-layouts  12.5 us (3%)
  matrix products  12 us (3%)
  other arithmetic  11.1 us (3%)
    psum x1, waiting for transfers between devices, shards(): summed = lax.psum(partial_field, 'mode')  190 us
    psum x1, blocking collectives, shards(): loop_momentum = lax.psum(padded, ('site', 'mode'))  105 us
    pallas_call x1, Pallas kernels, shift(): pl.pallas_call(relay, out_shape=jax.ShapeDtypeStruct((8, 128), jnp.float3...  14.9 us
    reduce_sum x1, other arithmetic, shards(): jnp.sum(weights[:, None, None] * cross, axis=0).reshape(4, 4, count)  8.7 us
  transfers between devices with their start and end apart: 1, of which 1 were waited for; matrix products, arithmetic and copies ran while one was open for 1% of the time, Pallas kernels for 4%

profile of v1, /device:TPU:1, one launch (start us, length us, event | category | flops | bytes accessed | tf_op | source)
XLA Modules:
  0.0 361.4 jit_solution(12726858088625437074)
XLA Ops:
  7.2 0.0 all-reduce.2.cloned.1.call-start
  7.2 2.7 copy.12
  9.9 2.7 reshape.277
  12.6 0.0 copy-start.4
  12.6 2.1 fusion.10
  14.7 0.0 copy-done.4
  14.7 8.7 %multiply_reduce_fusion = (f32[4,4,13824]{2,1,0:T(4,128)S(1)}, f32[4,4,13824]{2,1,0:T(4,128)S(1)}) fusion(f32[4,4,13824]{2,1,0:T(4,128)S(1)} %get-tuple-element.11, f32[4,4,13824]{2,1,0:T(4,128)S(1)} %get-tuple-element.12, f32[4,4,13824]{2,1,0:T(4,128)S(1)} %get-tuple-element.13, f32[4,4,13824]{2,1,0:T(4,128)S(1)} %get-tuple-element.14, ...), kind=kLoop, calls=%fused_computation.2 | loop fusion | flops 22560768 | bytes 7077904 | tf_op jit(solution)/shard_map/reduce_sum | solution.py:137
  23.4 0.0 copy-start
  23.4 0.0 copy-start.1
  23.4 0.3 reduce_sum.23
  23.8 0.3 reduce_sum.25
  24.1 0.1 copy-done
  24.1 1.5 fusion.48
  25.7 0.0 copy-done.1
  25.7 1.5 fusion
  27.2 0.0 copy-start.2
  27.2 0.0 copy-start.3
  27.2 1.7 reshape.278
  28.9 0.0 all-reduce.2.cloned.1.call-update
  28.9 0.0 copy-done.2
  28.9 0.5 slice.48
  30.1 0.6 add.166.x_ref
  30.7 14.9 %shard_map.68 = f32[8,128]{1,0:T(8,128)} custom-call(f32[8,128]{1,0:T(8,128)} %add.166.x_ref), custom_call_target="tpu_custom_call" | custom-call | tf_op jit(solution)/shard_map/pallas_call | solution.py:99
  45.6 1.2 slice.49
  47.5 0.0 copy-done.3
  47.5 0.1 add_bitcast_fusion
  47.6 0.1 add_bitcast_fusion.1
  47.7 0.1 add_bitcast_fusion.2
  47.8 190.4 %all-reduce.2.cloned.1.call-done = f32[2,16,4,27,128]{4,3,2,1,0:T(8,128)} async-done(((f32[2,16,4,27,128]{4,3,2,1,0:T(8,128)}), f32[2,16,4,27,128]{4,3,2,1,0:T(8,128)}) %all-reduce.2.cloned.1.call-update) | async-done | bytes 1769488 | tf_op jit(solution)/shard_map/psum | solution.py:145
  238.2 0.9 dynamic-slice_bitcast_fusion.1
  239.0 2.2 fusion.18
  241.3 2.2 fusion.16
  243.5 2.3 fusion.2
  245.8 2.2 fusion.1
  248.1 104.9 %psum.15 = f32[2,16,4,27]{3,2,1,0:T(4,128)} all-reduce(f32[2,16,4,27]{3,2,1,0:T(4,128)S(1)} %fusion.31), channel_id=1, replica_groups=mesh['site'=32,'mode'=16] {'site','mode'}, use_global_device_ids=true, to_apply=%region_3.4 | all-reduce | flops 3456 | bytes 27648 | tf_op jit(solution)/shard_map/psum | solution.py:154
  353.0 0.9 constant_dynamic-slice_fusion
  353.9 0.7 copy.13
  (7 shorter events, 0.1 us)
Async XLA Ops:
  7.2 231.0 %all-reduce.2.cloned.1.call-start = ((), (), s32[]{:S(2)}) async-start(), calls=%async_computation | async-start | bytes 4194304 | tf_op jit(solution)/shard_map/psum | solution.py:145
  12.6 2.1 copy-start.4
  23.4 0.7 copy-start
  23.4 2.2 copy-start.1
  27.2 1.7 copy-start.2
  27.2 20.3 %copy-start.3 = (s32[27]{0:T(128)S(1)}, s32[27]{0:T(128)}, u32[]{:S(2)}) copy-start(s32[27]{0:T(128)} %param.7) | copy-start | bytes 328
Sparse Core Ops, SparseCore 0:
  29.0 209.0 all-reduce.1

commit v2 on v0

v2 whole, which is shorter than its diff:
```python
import math

import jax
import jax.numpy as jnp
import numpy as np
from jax import lax
from jax.experimental import pallas as pl
from jax.experimental.pallas import tpu as pltpu
from jax.sharding import PartitionSpec as P

MESH = pl.DeviceIdType.MESH
F32 = jnp.float32
L = 48
LINE = 8
ROWS = 108
PAD = 112
CUTS = ((0, 64), (64, 48))
ORDER = (7, 6, 0, 1, 5, 4, 3, 2)
EARLY = 4

TREE = {
    7: {0: 2, 1: 2, 2: 7, 3: 4, 4: 7, 5: 7, 6: 7},
    6: {0: 2, 1: 2, 2: 6, 3: 4, 4: 6, 5: 6},
    5: {0: 1, 1: 5, 2: 3, 3: 5, 4: 5},
    4: {0: 1, 1: 4, 2: 3, 3: 4},
    3: {0: 1, 1: 3, 2: 3},
    2: {0: 1, 1: 2},
    1: {0: 1},
}
SLOTS = 4


def children(owner, place):
    return sorted(k for k, to in TREE[owner].items() if to == place)


def pick(index, values):
    out = jnp.int32(values[0])
    for i in range(1, len(values)):
        if values[i] != values[0]:
            out = jnp.where(index == i, jnp.int32(values[i]), out)
    return out


def gammas():
    u = 1j
    first = np.array([[0, 0, 0, u], [0, 0, u, 0], [0, -u, 0, 0], [-u, 0, 0, 0]])
    second = np.array([[0, 0, 0, -1], [0, 0, 1, 0], [0, 1, 0, 0], [-1, 0, 0, 0]], dtype=complex)
    third = np.array([[0, 0, u, 0], [0, 0, 0, -u], [-u, 0, 0, 0], [0, u, 0, 0]])
    fourth = np.array([[0, 0, 1, 0], [0, 0, 0, 1], [1, 0, 0, 0], [0, 1, 0, 0]], dtype=complex)
    basis = [first, second, third, fourth]
    fifth = first @ second @ third @ fourth
    out = []
    for number in range(16):
        matrix = np.eye(4, dtype=complex)
        for bit in range(4):
            if number >> bit & 1:
                matrix = matrix @ basis[bit]
        out.append(matrix @ fifth)
    return out


def traces():
    out = []
    for matrix in gammas():
        terms = []
        for s in range(4):
            if matrix[s, s] != 0:
                terms.append((matrix[s, s], ("d", s, s)))
            for r in range(s + 1, 4):
                real, imag = matrix[s, r] + matrix[r, s], 1j * (matrix[s, r] - matrix[r, s])
                if real != 0:
                    terms.append((real, ("a", s, r)))
                if imag != 0:
                    terms.append((imag, ("b", s, r)))
        imaginary = all(c.real == 0 for c, _ in terms)
        values = [(c.imag if imaginary else c.real, name) for c, name in terms]
        out.append((imaginary, [(c > 0, abs(c) == 2, name) for c, name in values]))
    return out


TRACES = traces()


def cosine(index):
    turn = index - 48.0 * jnp.floor(index * (1.0 / 48.0) + 0.5)
    x = (12.0 - jnp.abs(turn)) * (math.pi / 24.0)
    y = x * x
    p = -1.0 / 39916800.0
    for c in (1.0 / 362880.0, -1.0 / 5040.0, 1.0 / 120.0, -1.0 / 6.0, 1.0):
        p = p * y + c
    return x * p


def kernel(
    ev, eig, bmap, mom, field_out, mom_out,
    buf, part, other, held, wide, narrow, phase, lanes, own_p, plane, line, both,
    load_sem, core_send, core_recv, tree_send, tree_recv, mom_send, mom_recv, greet,
):
    site, mode = lax.axis_index("site"), lax.axis_index("mode")
    place, core = mode // 2, mode % 2
    half, xy = site // 16, site % 16
    x, y = xy % 4, xy // 4
    height = half * LINE + place

    def at_z(step):
        z = lax.rem(height + step + 16, 16)
        return (z // LINE * 16 + xy, z % LINE * 2 + core)

    def at_plane(column):
        return (half * 16 + column, mode)

    def in_row(step):
        return at_plane(y * 4 + lax.rem(x + step, 4))

    def in_column(step):
        return at_plane(lax.rem(y + step, 4) * 4 + x)

    def signal(sem, device):
        pl.semaphore_signal(sem, inc=1, device_id=device, device_id_type=MESH)

    twin = (site, place * 2 + 1 - core)
    barrier = pltpu.get_barrier_semaphore()
    near = [twin] + [at_z(s) for s in (1, -1, 2, -2)] + [f(s) for f in (in_row, in_column) for s in (1, 2, 3)]
    for device in near:
        signal(barrier, device)

    loads = [
        pltpu.make_async_copy(ev.at[pl.ds(24 * m, 24)], buf.at[pl.ds(24 * m, 24)], load_sem.at[m]) for m in range(4)
    ]
    for copy in loads:
        copy.start()

    lanes[...] = jnp.zeros((8, 128), jnp.int32)
    lanes[0:3, 0:27] = mom[...]
    spread = lanes[...].astype(F32)
    spread = spread + pltpu.roll(spread, 32, 1)
    spread = spread + pltpu.roll(spread, 64, 1)
    along = [jnp.broadcast_to(spread[i : i + 1], (8, 128)) for i in range(3)]
    lane = lax.broadcasted_iota(jnp.int32, (8, 128), 1)
    row = lax.broadcasted_iota(jnp.int32, (8, 128), 0)
    quarter = jnp.where(lane < 32, 0.0, jnp.where(lane < 64, -12.0, jnp.where(lane < 96, 12.0, 0.0)))
    inner = along[2] * row.astype(F32) + quarter
    for i in range(16):
        values = cosine(inner + along[1] * float(i % 4) + along[0] * float(i // 4))
        top = values.astype(jnp.bfloat16).astype(F32)
        lanes_f = (values - top)
        wide[8 * i : 8 * i + 8] = top
        narrow[8 * i : 8 * i + 8] = lanes_f
    turn = jnp.where(lane < 64, 0.0, -12.0)
    upper = row < 4
    for i in range(14):
        one, two = bmap[2 * i], bmap[min(2 * i + 1, 26)]
        def both_rows(f):
            return jnp.where(upper, f(one), f(two)).astype(F32)
        angle = along[0] * both_rows(lambda q: 4 * (q // 72)) + along[1] * both_rows(lambda q: 4 * (q // 6 % 12))
        angle = angle + along[2] * both_rows(lambda q: 8 * (q % 6))
        phase[8 * i : 8 * i + 8] = cosine(angle + turn)
    weights = [1.0 / jnp.full((8, 128), eig[m], F32) for m in range(4)]
    for par in range(2):
        for q in range(8):
            part[par, q, 104:112] = jnp.zeros((8, 128), F32)

    def density(early, rows, load):
        pairs = ((0, 3), (1, 2)) if early else ((0, 1), (2, 3), (0, 2), (1, 3))
        names = [("d", s, s) for s in range(4)] if early else []
        names += [(kind, s, r) for s, r in pairs for kind in ("a", "b")]
        total = {}
        for m in range(4):
            weight = jnp.broadcast_to(weights[m][0:1], (rows, 128))
            inside = {}
            for c in range(3):
                real = [load(m * 24 + s * 3 + c) for s in range(4)]
                imag = [load(m * 24 + 12 + s * 3 + c) for s in range(4)]
                for kind, s, r in names:
                    if kind == "b":
                        value = real[s] * imag[r] - imag[s] * real[r]
                    else:
                        value = real[s] * real[r] + imag[s] * imag[r]
                    key = (kind, s, r)
                    inside[key] = inside[key] + value if c else value
            for key in names:
                value = weight * inside[key]
                total[key] = total[key] + value if m else value
        out = []
        for q in range(EARLY) if early else range(EARLY, 8):
            for par in range(2):
                terms = TRACES[2 * ORDER[q] + par][1]
                value = None
                for positive, _, name in terms:
                    if value is None:
                        value = total[name] if positive else -total[name]
                    else:
                        value = value + total[name] if positive else value - total[name]
                if terms[0][1]:
                    value = value + value
                out.append((par, q, value))
        return out

    def groups(early, first, last):
        def body(g, carry):
            base = pl.multiple_of(g * 16, 16)
            for par, q, value in density(early, 16, lambda p: buf[p, pl.ds(base, 16)].astype(F32)):
                part[par, q, pl.ds(base, 16)] = value
            return carry
        lax.fori_loop(first, last, body, 0)

    def tail(early):
        for par, q, value in density(early, 12, lambda p: buf[p, 96:108].astype(F32)):
            part[par, q, 96:108] = value

    def to_twin(stage, cut):
        start, size = CUTS[cut]
        return pltpu.make_async_remote_copy(
            src_ref=part.at[1 - core, pl.ds(4 * stage, 4), pl.ds(start, size)],
            dst_ref=other.at[pl.ds(4 * stage, 4), pl.ds(start, size)],
            send_sem=core_send.at[stage, cut], recv_sem=core_recv.at[stage, cut],
            device_id=twin, device_id_type=MESH,
        )

    def from_twin(stage, cut):
        to_twin(stage, cut).wait_recv()
        start, size = CUTS[cut]
        for q in range(4 * stage, 4 * stage + 4):
            part[core, q, start : start + size] += other[q, start : start + size]

    ways = (place, LINE - 1 - place)

    def owner_at(way, owner):
        return ORDER.index(owner if way == 0 else LINE - 1 - owner)

    def step_to(way, owner, cut, source):
        here = ways[way]
        parents = [TREE[owner].get(k, owner) for k in range(LINE)]
        slots = [children(owner, TREE[owner][k]).index(k) if k in TREE[owner] else 0 for k in range(LINE)]
        to = pick(here, parents)
        target = to if way == 0 else LINE - 1 - to
        start, size = CUTS[cut]
        slot = pick(here, slots)
        return pltpu.make_async_remote_copy(
            src_ref=source.at[pl.ds(start, size)],
            dst_ref=held.at[way, owner, slot, pl.ds(start, size)],
            send_sem=tree_send.at[way, owner], recv_sem=tree_recv.at[way, owner, slot, cut],
            device_id=(site, target * 2 + core), device_id_type=MESH,
        )

    def arrived(way, owner, slot, cut):
        start, size = CUTS[cut]
        ref = held.at[way, owner, slot, pl.ds(start, size)]
        pltpu.make_async_remote_copy(
            src_ref=ref, dst_ref=ref, send_sem=tree_send.at[way, owner], recv_sem=tree_recv.at[way, owner, slot, cut],
            device_id=twin, device_id_type=MESH,
        ).wait_recv()

    def leaves(way, owner):
        here = ways[way]
        return pick(here, [int(k < owner and not children(owner, k)) for k in range(LINE)]) == 1

    def collectors(way, owner):
        here = ways[way]
        return [(n, pick(here, [int(k < owner and len(children(owner, k)) > n) for k in range(LINE)]) == 1)
                for n in range(max(len(children(owner, k)) for k in range(owner)))]

    def send_leaves(owner, cut):
        for way in range(2):
            @pl.when(leaves(way, owner))
            def _():
                step_to(way, owner, cut, part.at[core, owner_at(way, owner)]).start()

    def send_collected(owner, cut):
        start, size = CUTS[cut]
        for way in range(2):
            slots = collectors(way, owner)
            if not slots:
                continue

            @pl.when(slots[0][1])
            def _():
                for n, here in slots:
                    if n == 0:
                        arrived(way, owner, 0, cut)
                        held[way, owner, 0, start : start + size] += part[core, owner_at(way, owner), start : start + size]
                    else:
                        @pl.when(here)
                        def _():
                            arrived(way, owner, n, cut)
                            held[way, owner, 0, start : start + size] += held[way, owner, n, start : start + size]
                step_to(way, owner, cut, held.at[way, owner, 0]).start()

    for copy in loads:
        copy.wait()
    groups(True, 0, 4)
    pl.semaphore_wait(barrier, len(near))
    for i, device in enumerate([in_column(1), in_column(2), in_column(3), at_z(2), at_z(-2)]):
        signal(greet.at[i], device)
    to_twin(0, 0).start()
    groups(True, 4, 6)
    tail(True)
    to_twin(0, 1).start()
    groups(False, 0, 4)
    to_twin(1, 0).start()
    for cut in range(2):
        from_twin(0, cut)
        for owner in (7, 6):
            send_leaves(owner, cut)
    groups(False, 4, 6)
    tail(False)
    to_twin(1, 1).start()
    for cut in range(2):
        from_twin(1, cut)
        for owner in (5, 4, 3, 2):
            send_leaves(owner, cut)
    for cut in range(2):
        send_leaves(1, cut)
    for i in range(5):
        pl.semaphore_wait(greet.at[i], 1)
    for i, device in enumerate([at_z(1), at_z(-1), at_z(4), at_z(-4)]):
        signal(greet.at[5 + i], device)

    top = wide[...].astype(jnp.bfloat16)
    rest = narrow[...].astype(jnp.bfloat16)
    doubled = jnp.concatenate([top, top], axis=0)

    def project(q, carry):
        share = part[core, q]
        high = share.astype(jnp.bfloat16)
        low = (share - high.astype(F32)).astype(jnp.bfloat16)
        value = jnp.dot(jnp.concatenate([high, low], axis=1), doubled, preferred_element_type=F32)
        value = value + jnp.dot(high, rest, preferred_element_type=F32)
        own_p[q] = (value * phase[...]).reshape(14, 8, 128).sum(axis=0)
        return carry

    lax.fori_loop(0, 8, project, 0)
    folded = []
    for q in range(8):
        value = own_p[q]
        value = value + pltpu.roll(value, 4, 0)
        folded.append(value + pltpu.roll(value, 64, 1))
    for i in range(2):
        pairs = [jnp.where(upper, folded[4 * i + 2 * j], folded[4 * i + 2 * j + 1]) for j in range(2)]
        plane[xy, 8 * i : 8 * i + 8] = jnp.where(lane < 64, pairs[0], pairs[1])

    def share_out(buffer, slot, stage, devices):
        for device in devices:
            pltpu.make_async_remote_copy(
                src_ref=buffer.at[slot], dst_ref=buffer.at[slot], send_sem=mom_send.at[stage], recv_sem=mom_recv.at[stage],
                device_id=device, device_id_type=MESH,
            ).start()

    def gathered(buffer, count, stage):
        ref = buffer.at[pl.ds(0, count)]
        return pltpu.make_async_remote_copy(
            src_ref=ref, dst_ref=ref, send_sem=mom_send.at[stage], recv_sem=mom_recv.at[stage],
            device_id=twin, device_id_type=MESH,
        )

    share_out(plane, xy, 0, [at_plane(lax.rem(xy + s, 16)) for s in range(1, 16)])

    for owner in (7, 6):
        for cut in range(2):
            if owner == 7 and cut == 0:
                for i in (5, 6):
                    pl.semaphore_wait(greet.at[i], 1)
            send_collected(owner, cut)
    for owner in (5, 4, 3, 2):
        for cut in range(2):
            send_collected(owner, cut)

    gathered(plane, 15, 0).wait_recv()
    value = plane[0]
    for i in range(1, 16):
        value = value + plane[i]
    line[height] = value
    for i in (7, 8):
        pl.semaphore_wait(greet.at[i], 1)
    share_out(line, height, 1, [at_z(s) for s in (8, 7, -7, 6, -6, 5, -5, 4, -4, 3, -3, 2, -2, 1, -1)])

    mine = pick(place, [ORDER.index(p) for p in range(LINE)])
    for cut, (start, size) in enumerate(CUTS):
        rows = pl.ds(start, size)
        for way in range(2):
            for owner in range(1, LINE):
                count = len(children(owner, owner))
                @pl.when(ways[way] == owner)
                def _():
                    for n in range(count):
                        arrived(way, owner, n, cut)
                        part[core, mine, rows] += held[way, owner, n, start : start + size]
    total = part[core, mine]
    imaginary = pick(mode, [int(t[0]) for t in TRACES]) == 1
    field_out[0:ROWS] = jnp.where(imaginary, 0.0, total)[0:ROWS]
    field_out[ROWS : 2 * ROWS] = jnp.where(imaginary, total, 0.0)[0:ROWS]

    gathered(line, 15, 1).wait_recv()
    value = line[0]
    for i in range(1, 16):
        value = value + line[i]
    both[core] = value * (L**-1.5)
    cross = pltpu.make_async_remote_copy(
        src_ref=both.at[core], dst_ref=both.at[core], send_sem=mom_send.at[2], recv_sem=mom_recv.at[2],
        device_id=twin, device_id_type=MESH,
    )
    cross.start()

    for stage in range(2):
        for cut in range(2):
            to_twin(stage, cut).wait_send()
        gathered((plane, line)[stage], 15, stage).wait_send()
    for way in range(2):
        for owner in range(1, LINE):
            @pl.when(ways[way] < owner)
            def _():
                ref = held.at[way, owner, 0]
                pltpu.make_async_remote_copy(
                    src_ref=ref, dst_ref=ref, send_sem=tree_send.at[way, owner], recv_sem=tree_recv.at[way, owner, 0, 0],
                    device_id=twin, device_id_type=MESH,
                ).wait_send()
    cross.wait()
    for par in range(2):
        value = both[par]
        turned = [value] + [pltpu.roll(value, 128 - s, 1) for s in (32, 64, 96)]
        for q in range(8):
            n = 2 * ORDER[q] + par
            first = 8 * (q // 4) + 4 * (q % 2)
            c, s = (turned[2 * (q % 4 // 2) + j][first : first + 4, 0:27] for j in range(2))
            mom_out[0, n] = s if TRACES[n][0] else c
            mom_out[1, n] = c if TRACES[n][0] else -s


def shards(eigvecs, eigenvalues, block_map, momenta):
    vectors = eigvecs.transpose(0, 1, 2, 3, 5, 4, 6)

    def body(ev, *refs):
        kernel(ev.reshape(96, ROWS, 128), *refs)

    dma, vmem = pltpu.SemaphoreType.DMA, pltpu.VMEM
    field, sums = pl.pallas_call(
        body,
        out_shape=(jax.ShapeDtypeStruct((2 * ROWS, 128), F32), jax.ShapeDtypeStruct((2, 16, 4, 27), F32)),
        in_specs=[
            pl.BlockSpec(memory_space=pl.ANY),
            pl.BlockSpec(memory_space=pltpu.SMEM),
            pl.BlockSpec(memory_space=pltpu.SMEM),
            pl.BlockSpec(memory_space=pltpu.VMEM),
        ],
        out_specs=(pl.BlockSpec(memory_space=pltpu.VMEM), pl.BlockSpec(memory_space=pltpu.VMEM)),
        scratch_shapes=[
            vmem((96, ROWS, 128), jnp.bfloat16),
            vmem((2, 8, PAD, 128), F32),
            vmem((8, PAD, 128), F32),
            vmem((2, LINE, SLOTS, PAD, 128), F32),
            vmem((128, 128), F32),
            vmem((128, 128), F32),
            vmem((PAD, 128), F32),
            vmem((8, 128), jnp.int32),
            vmem((8, 8, 128), F32),
            vmem((16, 16, 128), F32),
            vmem((16, 16, 128), F32),
            vmem((2, 16, 128), F32),
            dma((4,)),
            dma((2, 2)),
            dma((2, 2)),
            dma((2, LINE)),
            dma((2, LINE, SLOTS, 2)),
            dma((3,)),
            dma((3,)),
            pltpu.SemaphoreType.REGULAR((9,)),
        ],
        compiler_params=pltpu.CompilerParams(collective_id=0, has_side_effects=True, vmem_limit_bytes=56 * 2**20),
        name="loops",
    )(vectors, eigenvalues, block_map, momenta.T)
    field = field.reshape(2, 1, 27, 4, 128).transpose(0, 1, 3, 2, 4)
    return field, sums


def solution(mesh):
    placed = (P("mode", None, None, None, None, "site", None), P("mode"), P("site"), P())
    return jax.shard_map(
        shards,
        mesh=mesh,
        in_specs=placed,
        out_specs=(P(None, "mode", None, "site", None), P()),
        check_vma=False,
    )
```

time: 362 us -> 45.4 us (0.13)
  waiting for transfers between devices: 209 us -> 0 us
  blocking collectives: 105 us -> 0 us
  Pallas kernels: 0 us -> 41.5 us
  between operations: 14.2 us -> 0.64 us
  matrix products: 12 us -> 0 us
  other arithmetic: 11.1 us -> 0 us
  local copies, waits for them, and re-layouts: 10.2 us -> 3.02 us
    psum x1 -> x0, waiting for transfers between devices: 209 us -> none  [shards(): summed = lax.psum(partial_field, 'mode')]
    psum x1 -> x0, blocking collectives: 105 us -> none  [shards(): loop_momentum = lax.psum(padded, ('site', 'mode'))]
    pallas_call x0 -> x1, Pallas kernels: none -> 41.5 us  [shards(): pl.pallas_call(body, out_shape=(jax.ShapeDtypeStruct((2 * ROWS, 128), F32...]
    dot_general x6 -> x0, matrix products: 12 us -> none  [the longest x2 3.02 us: shards(): jnp.einsum('nk,kx->nx', table, flat, precision=hp)]
    reduce_sum x1 -> x0, other arithmetic: 8.7 us -> none  [shards(): jnp.sum(weights[:, None, None] * cross, axis=0).reshape(4, 4, count)]
    reshape x2 -> x0, local copies, waits for them, and re-layouts: 4.32 us -> none  [the longest x1 2.66 us: shards(): values = eigvecs.reshape(local_modes, 2, 4, 3, count)]
  transfers between devices with their start and end apart: 1 -> 0, of which waited for: 1 -> 0; matrix products, arithmetic and copies ran while one was open for 0% -> 0% of each run, Pallas kernels for 0% -> 0%
where the time goes in v2:
time: 45.4 us; the launch traced here: 45.1 us
  Pallas kernels  41.5 us (91%)
  local copies, waits for them, and re-layouts  3.02 us (7%)
  between operations  0.64 us (1%)
    pallas_call x1, Pallas kernels, shards(): pl.pallas_call(body, out_shape=(jax.ShapeDtypeStruct((2 * ROWS, 128), F32...  41.5 us
    unnamed x2, local copies, waits for them, and re-layouts  3.02 us

profile of v2, /device:TPU:1, one launch (start us, length us, event | category | flops | bytes accessed | tf_op | source)
XLA Modules:
  0.0 45.1 jit_solution(1994757161177256596)
XLA Ops:
  0.6 41.5 %loops.1 = (f32[216,128]{1,0:T(8,128)}, f32[2,16,4,27]{3,2,1,0:T(4,128)}) custom-call(bf16[4,2,4,3,27,4,128]{6,5,4,3,2,1,0:T(4,128)(2,1)} %bitcast.7, f32[4]{0:T(128)} %refs_0_.1, s32[27]{0:T(128)} %refs_1_.1, s32[3,27]{1,0:T(4,128)} %bitcast.9), custom_call_target="tpu_custom_call" | custom-call | tf_op jit(solution)/shard_map/loops/pallas_call | solution.py:437
  42.1 1.5 %copy.9 = f32[2,1,4,27,128]{4,2,3,1,0:T(4,128)} copy(f32[2,1,4,27,128]{4,2,3,1,0:T(4,128)} %bitcast.8) | data formatting | bytes 221184
  43.7 1.5 %copy.10 = f32[2,16,4,27]{3,2,1,0:T(4,128)} copy(f32[2,16,4,27]{3,2,1,0:T(4,128)} %get-tuple-element.9) | data formatting | bytes 27648

commit v3 on v2

--- a/solution.py
+++ b/solution.py
@@ -16,6 +16,7 @@
 PAD = 112
 CUTS = ((0, 64), (64, 48))
 ORDER = (7, 6, 0, 1, 5, 4, 3, 2)
+ROOTS = 2
 EARLY = 4
 
 TREE = {
@@ -93,14 +94,13 @@
 
 
 def kernel(
-    ev, eig, bmap, mom, field_out, mom_out,
-    buf, part, other, held, wide, narrow, phase, lanes, own_p, plane, line, both,
+    ev, eig_in, bmap_in, mom_in, field_out, mom_out,
+    buf, part, other, held, wide, narrow, phase, lanes, plane, line, both, eig, bmap, mom,
     load_sem, core_send, core_recv, tree_send, tree_recv, mom_send, mom_recv, greet,
 ):
     site, mode = lax.axis_index("site"), lax.axis_index("mode")
     place, core = mode // 2, mode % 2
     half, xy = site // 16, site % 16
-    x, y = xy % 4, xy // 4
     height = half * LINE + place
 
     def at_z(step):
@@ -110,20 +110,35 @@
     def at_plane(column):
         return (half * 16 + column, mode)
 
-    def in_row(step):
-        return at_plane(y * 4 + lax.rem(x + step, 4))
-
-    def in_column(step):
-        return at_plane(lax.rem(y + step, 4) * 4 + x)
-
     def signal(sem, device):
         pl.semaphore_signal(sem, inc=1, device_id=device, device_id_type=MESH)
 
     twin = (site, place * 2 + 1 - core)
     barrier = pltpu.get_barrier_semaphore()
-    near = [twin] + [at_z(s) for s in (1, -1, 2, -2)] + [f(s) for f in (in_row, in_column) for s in (1, 2, 3)]
-    for device in near:
-        signal(barrier, device)
+    small = [
+        pltpu.make_async_copy(source, target, load_sem.at[4 + i])
+        for i, (source, target) in enumerate(((eig_in, eig), (bmap_in, bmap), (mom_in, mom)))
+    ]
+    for copy in small:
+        copy.start()
+    near = (1, -1, 2, -2)
+    root = height < ROOTS
+    signal(barrier, twin)
+    for step in near:
+        signal(barrier, at_z(step))
+    expected = jnp.int32(1 + len(near))
+    for r in range(ROOTS):
+        apart = lax.rem(height - r + 16, 16)
+        expected = expected + jnp.where((apart > 2) & (apart < 14), 1, 0)
+
+    @pl.when(root)
+    def _():
+        for step in range(3, 14):
+            signal(barrier, at_z(step))
+        for step in range(1, 16):
+            signal(barrier, at_plane(lax.rem(xy + step, 16)))
+
+    expected = expected + jnp.where(root, 15, 0)
 
     loads = [
         pltpu.make_async_copy(ev.at[pl.ds(24 * m, 24)], buf.at[pl.ds(24 * m, 24)], load_sem.at[m]) for m in range(4)
@@ -131,6 +146,8 @@
     for copy in loads:
         copy.start()
 
+    for copy in small:
+        copy.wait()
     lanes[...] = jnp.zeros((8, 128), jnp.int32)
     lanes[0:3, 0:27] = mom[...]
     spread = lanes[...].astype(F32)
@@ -287,12 +304,43 @@
                             held[way, owner, 0, start : start + size] += held[way, owner, n, start : start + size]
                 step_to(way, owner, cut, held.at[way, owner, 0]).start()
 
+    top = wide[...].astype(jnp.bfloat16)
+    rest = narrow[...].astype(jnp.bfloat16)
+    doubled = jnp.concatenate([top, top], axis=0)
+
+    def project(stage):
+        share = part[core, 4 * stage : 4 * stage + 4].reshape(4 * PAD, 128)
+        high = share.astype(jnp.bfloat16)
+        low = (share - high.astype(F32)).astype(jnp.bfloat16)
+        value = jnp.dot(jnp.concatenate([high, low], axis=1), doubled, preferred_element_type=F32)
+        value = value + jnp.dot(high, rest, preferred_element_type=F32)
+        value = (value.reshape(4, PAD, 128) * phase[...][None]).reshape(4, 14, 8, 128).sum(axis=1)
+        folded = []
+        for q in range(4):
+            one = value[q] + pltpu.roll(value[q], 4, 0)
+            folded.append(one + pltpu.roll(one, 64, 1))
+        pairs = [jnp.where(upper, folded[2 * j], folded[2 * j + 1]) for j in range(2)]
+        line[height, 8 * stage : 8 * stage + 8] = jnp.where(lane < 64, pairs[0], pairs[1])
+
+    def passed(buffer, slot, stage, device):
+        return pltpu.make_async_remote_copy(
+            src_ref=buffer.at[slot], dst_ref=buffer.at[slot], send_sem=mom_send.at[stage], recv_sem=mom_recv.at[stage],
+            device_id=device, device_id_type=MESH,
+        )
+
+    def whole(buffer, count, stage):
+        ref = buffer.at[pl.ds(0, count)]
+        return pltpu.make_async_remote_copy(
+            src_ref=ref, dst_ref=ref, send_sem=mom_send.at[stage], recv_sem=mom_recv.at[stage],
+            device_id=twin, device_id_type=MESH,
+        )
+
     for copy in loads:
         copy.wait()
     groups(True, 0, 4)
-    pl.semaphore_wait(barrier, len(near))
-    for i, device in enumerate([in_column(1), in_column(2), in_column(3), at_z(2), at_z(-2)]):
-        signal(greet.at[i], device)
+    pl.semaphore_wait(barrier, expected)
+    for i, step in enumerate((2, -2)):
+        signal(greet.at[i], at_z(step))
     to_twin(0, 0).start()
     groups(True, 4, 6)
     tail(True)
@@ -306,74 +354,41 @@
     groups(False, 4, 6)
     tail(False)
     to_twin(1, 1).start()
+    project(0)
     for cut in range(2):
         from_twin(1, cut)
-        for owner in (5, 4, 3, 2):
+    project(1)
+    for r in range(ROOTS):
+        @pl.when(height != r)
+        def _():
+            passed(line, height, 0, (xy, 2 * r + core)).start()
+    for owner in (5, 4, 3, 2, 1):
+        for cut in range(2):
             send_leaves(owner, cut)
-    for cut in range(2):
-        send_leaves(1, cut)
-    for i in range(5):
+
+    for i in range(2):
         pl.semaphore_wait(greet.at[i], 1)
-    for i, device in enumerate([at_z(1), at_z(-1), at_z(4), at_z(-4)]):
-        signal(greet.at[5 + i], device)
-
-    top = wide[...].astype(jnp.bfloat16)
-    rest = narrow[...].astype(jnp.bfloat16)
-    doubled = jnp.concatenate([top, top], axis=0)
-
-    def project(q, carry):
-        share = part[core, q]
-        high = share.astype(jnp.bfloat16)
-        low = (share - high.astype(F32)).astype(jnp.bfloat16)
-        value = jnp.dot(jnp.concatenate([high, low], axis=1), doubled, preferred_element_type=F32)
-        value = value + jnp.dot(high, rest, preferred_element_type=F32)
-        own_p[q] = (value * phase[...]).reshape(14, 8, 128).sum(axis=0)
-        return carry
-
-    lax.fori_loop(0, 8, project, 0)
-    folded = []
-    for q in range(8):
-        value = own_p[q]
-        value = value + pltpu.roll(value, 4, 0)
-        folded.append(value + pltpu.roll(value, 64, 1))
-    for i in range(2):
-        pairs = [jnp.where(upper, folded[4 * i + 2 * j], folded[4 * i + 2 * j + 1]) for j in range(2)]
-        plane[xy, 8 * i : 8 * i + 8] = jnp.where(lane < 64, pairs[0], pairs[1])
-
-    def share_out(buffer, slot, stage, devices):
-        for device in devices:
-            pltpu.make_async_remote_copy(
-                src_ref=buffer.at[slot], dst_ref=buffer.at[slot], send_sem=mom_send.at[stage], recv_sem=mom_recv.at[stage],
-                device_id=device, device_id_type=MESH,
-            ).start()
-
-    def gathered(buffer, count, stage):
-        ref = buffer.at[pl.ds(0, count)]
-        return pltpu.make_async_remote_copy(
-            src_ref=ref, dst_ref=ref, send_sem=mom_send.at[stage], recv_sem=mom_recv.at[stage],
-            device_id=twin, device_id_type=MESH,
-        )
-
-    share_out(plane, xy, 0, [at_plane(lax.rem(xy + s, 16)) for s in range(1, 16)])
-
-    for owner in (7, 6):
+    for i, step in enumerate((1, -1)):
+        signal(greet.at[2 + i], at_z(step))
+    for owner in (7, 6, 5, 4, 3, 2):
         for cut in range(2):
             if owner == 7 and cut == 0:
-                for i in (5, 6):
-                    pl.semaphore_wait(greet.at[i], 1)
+                for i in range(2):
+                    pl.semaphore_wait(greet.at[2 + i], 1)
             send_collected(owner, cut)
-    for owner in (5, 4, 3, 2):
-        for cut in range(2):
-            send_collected(owner, cut)
-
-    gathered(plane, 15, 0).wait_recv()
-    value = plane[0]
-    for i in range(1, 16):
-        value = value + plane[i]
-    line[height] = value
-    for i in (7, 8):
-        pl.semaphore_wait(greet.at[i], 1)
-    share_out(line, height, 1, [at_z(s) for s in (8, 7, -7, 6, -6, 5, -5, 4, -4, 3, -3, 2, -2, 1, -1)])
+
+    def added(buffer):
+        value = buffer[0]
+        for i in range(1, 16):
+            value = value + buffer[i]
+        return value
+
+    @pl.when(root)
+    def _():
+        whole(line, 15, 0).wait_recv()
+        plane[xy] = added(line)
+        for step in range(1, 16):
+            passed(plane, xy, 1, at_plane(lax.rem(xy + step, 16))).start()
 
     mine = pick(place, [ORDER.index(p) for p in range(LINE)])
     for cut, (start, size) in enumerate(CUTS):
@@ -391,21 +406,44 @@
     field_out[0:ROWS] = jnp.where(imaginary, 0.0, total)[0:ROWS]
     field_out[ROWS : 2 * ROWS] = jnp.where(imaginary, total, 0.0)[0:ROWS]
 
-    gathered(line, 15, 1).wait_recv()
-    value = line[0]
-    for i in range(1, 16):
-        value = value + line[i]
-    both[core] = value * (L**-1.5)
-    cross = pltpu.make_async_remote_copy(
-        src_ref=both.at[core], dst_ref=both.at[core], send_sem=mom_send.at[2], recv_sem=mom_recv.at[2],
-        device_id=twin, device_id_type=MESH,
-    )
-    cross.start()
+    def spread_out(start):
+        for r in range(ROOTS):
+            @pl.when(height == r)
+            def _():
+                for z in (8, 9, 10, 11, 12, 13, 14, 15) if r == 0 else (7, 6, 5, 4, 3, 2):
+                    for c in range(2):
+                        copy = passed(both, core, 2, (z // LINE * 16 + xy, z % LINE * 2 + c))
+                        copy.start() if start else copy.wait_send()
+
+    @pl.when(root)
+    def _():
+        whole(plane, 15, 1).wait_recv()
+        both[core] = added(plane) * (L**-1.5)
+        passed(both, core, 2, twin).start()
+        spread_out(True)
+        passed(both, core, 2, twin).wait_recv()
+
+    @pl.when(jnp.logical_not(root))
+    def _():
+        whole(both, 2, 2).wait_recv()
+
+    for par in range(2):
+        value = both[par]
+        turned = [value] + [pltpu.roll(value, 128 - s, 1) for s in (32, 64, 96)]
+        for q in range(8):
+            n = 2 * ORDER[q] + par
+            first = 8 * (q // 4) + 4 * (q % 2)
+            c, s = (turned[2 * (q % 4 // 2) + j][first : first + 4, 0:27] for j in range(2))
+            mom_out[0, n] = s if TRACES[n][0] else c
+            mom_out[1, n] = c if TRACES[n][0] else -s
 
     for stage in range(2):
         for cut in range(2):
             to_twin(stage, cut).wait_send()
-        gathered((plane, line)[stage], 15, stage).wait_send()
+    for r in range(ROOTS):
+        @pl.when(height != r)
+        def _():
+            passed(line, height, 0, twin).wait_send()
     for way in range(2):
         for owner in range(1, LINE):
             @pl.when(ways[way] < owner)
@@ -415,16 +453,23 @@
                     src_ref=ref, dst_ref=ref, send_sem=tree_send.at[way, owner], recv_sem=tree_recv.at[way, owner, 0, 0],
                     device_id=twin, device_id_type=MESH,
                 ).wait_send()
-    cross.wait()
-    for par in range(2):
-        value = both[par]
-        turned = [value] + [pltpu.roll(value, 128 - s, 1) for s in (32, 64, 96)]
-        for q in range(8):
-            n = 2 * ORDER[q] + par
-            first = 8 * (q // 4) + 4 * (q % 2)
-            c, s = (turned[2 * (q % 4 // 2) + j][first : first + 4, 0:27] for j in range(2))
-            mom_out[0, n] = s if TRACES[n][0] else c
-            mom_out[1, n] = c if TRACES[n][0] else -s
+
+    @pl.when(root)
+    def _():
+        whole(plane, 15, 1).wait_send()
+        passed(both, core, 2, twin).wait_send()
+        spread_out(False)
+
+
+def deliver(field_in, mom_in, field_out, mom_out, sem):
+    copies = [
+        pltpu.make_async_copy(field_in, field_out, sem.at[0]),
+        pltpu.make_async_copy(mom_in, mom_out, sem.at[1]),
+    ]
+    for copy in copies:
+        copy.start()
+    for copy in copies:
+        copy.wait()
 
 
 def shards(eigvecs, eigenvalues, block_map, momenta):
@@ -434,15 +479,12 @@
         kernel(ev.reshape(96, ROWS, 128), *refs)
 
     dma, vmem = pltpu.SemaphoreType.DMA, pltpu.VMEM
+    anywhere = pl.BlockSpec(memory_space=pl.ANY)
+    shapes = ((2 * ROWS, 128), (2, 16, 4, 27))
     field, sums = pl.pallas_call(
         body,
-        out_shape=(jax.ShapeDtypeStruct((2 * ROWS, 128), F32), jax.ShapeDtypeStruct((2, 16, 4, 27), F32)),
-        in_specs=[
-            pl.BlockSpec(memory_space=pl.ANY),
-            pl.BlockSpec(memory_space=pltpu.SMEM),
-            pl.BlockSpec(memory_space=pltpu.SMEM),
-            pl.BlockSpec(memory_space=pltpu.VMEM),
-        ],
+        out_shape=tuple(pltpu.VMEM(shape, F32) for shape in shapes),
+        in_specs=[pl.BlockSpec(memory_space=pltpu.HBM)] * 4,
         out_specs=(pl.BlockSpec(memory_space=pltpu.VMEM), pl.BlockSpec(memory_space=pltpu.VMEM)),
         scratch_shapes=[
             vmem((96, ROWS, 128), jnp.bfloat16),
@@ -453,22 +495,32 @@
             vmem((128, 128), F32),
             vmem((PAD, 128), F32),
             vmem((8, 128), jnp.int32),
-            vmem((8, 8, 128), F32),
             vmem((16, 16, 128), F32),
             vmem((16, 16, 128), F32),
             vmem((2, 16, 128), F32),
-            dma((4,)),
+            pltpu.SMEM((4,), F32),
+            pltpu.SMEM((27,), jnp.int32),
+            vmem((3, 27), jnp.int32),
+            dma((7,)),
             dma((2, 2)),
             dma((2, 2)),
             dma((2, LINE)),
             dma((2, LINE, SLOTS, 2)),
             dma((3,)),
             dma((3,)),
-            pltpu.SemaphoreType.REGULAR((9,)),
+            pltpu.SemaphoreType.REGULAR((4,)),
         ],
         compiler_params=pltpu.CompilerParams(collective_id=0, has_side_effects=True, vmem_limit_bytes=56 * 2**20),
         name="loops",
     )(vectors, eigenvalues, block_map, momenta.T)
+    field, sums = pl.pallas_call(
+        deliver,
+        out_shape=tuple(jax.ShapeDtypeStruct(shape, F32) for shape in shapes),
+        in_specs=[pl.BlockSpec(memory_space=pltpu.VMEM)] * 2,
+        out_specs=(anywhere, anywhere),
+        scratch_shapes=[dma((2,))],
+        name="deliver",
+    )(*(pltpu.with_memory_space_constraint(a, pltpu.VMEM) for a in (field, sums)))
     field = field.reshape(2, 1, 27, 4, 128).transpose(0, 1, 3, 2, 4)
     return field, sums
 

time: 45.4 us -> 37.1 us (0.82)
  Pallas kernels: 41.5 us -> 36.3 us
  local copies, waits for them, and re-layouts: 3.02 us -> 0 us
    pallas_call x1 -> x2, Pallas kernels: 41.5 us -> 36.3 us  [the longest x1 35.6 us: shards(): pl.pallas_call(body, out_shape=tuple((pltpu.VMEM(shape, F32) for shape in...]
    unnamed x2 -> x0, local copies, waits for them, and re-layouts: 3.02 us -> none
where the time goes in v3:
time: 37.1 us; the launch traced here: 37 us
  Pallas kernels  36.3 us (98%)
  between operations  0.64 us (2%)
    pallas_call x1, Pallas kernels, shards(): pl.pallas_call(body, out_shape=tuple((pltpu.VMEM(shape, F32) for shape in...  35.6 us

profile of v3, /device:TPU:1, one launch (start us, length us, event | category | flops | bytes accessed | tf_op | source)
XLA Modules:
  0.0 37.0 jit_solution(8554762841628816573)
XLA Ops:
  0.6 35.6 %loops.1 = (f32[216,128]{1,0:T(8,128)S(1)}, f32[2,16,4,27]{3,2,1,0:T(4,128)S(1)}) custom-call(bf16[4,2,4,3,27,4,128]{6,5,4,3,2,1,0:T(4,128)(2,1)} %bitcast.7, f32[4]{0:T(128)} %refs_0_.1, s32[27]{0:T(128)} %refs_1_.1, s32[3,27]{1,0:T(4,128)} %bitcast.8), custom_call_target="tpu_custom_call" | custom-call | tf_op jit(solution)/shard_map/loops/pallas_call | solution.py:484
  36.3 0.7 %deliver.1 = (f32[216,128]{1,0:T(8,128)}, f32[2,16,4,27]{3,2,1,0:T(4,128)}) custom-call(f32[216,128]{1,0:T(8,128)S(1)} %get-tuple-element.6.field_in, f32[2,16,4,27]{3,2,1,0:T(4,128)S(1)} %get-tuple-element.7.mom_in), custom_call_target="tpu_custom_call" | custom-call | tf_op jit(solution)/shard_map/deliver/pallas_call | solution.py:516

commit v4 on v3

--- a/solution.py
+++ b/solution.py
@@ -16,12 +16,13 @@
 PAD = 112
 CUTS = ((0, 64), (64, 48))
 ORDER = (7, 6, 0, 1, 5, 4, 3, 2)
+PAIRS = tuple((s, r) for s in range(4) for r in range(s + 1, 4))
+NAMES = tuple(("d", s, s) for s in range(4)) + tuple((kind, s, r) for s, r in PAIRS for kind in ("a", "b"))
 ROOTS = 2
-EARLY = 4
 
 TREE = {
-    7: {0: 2, 1: 2, 2: 7, 3: 4, 4: 7, 5: 7, 6: 7},
-    6: {0: 2, 1: 2, 2: 6, 3: 4, 4: 6, 5: 6},
+    7: {0: 1, 1: 7, 2: 3, 3: 7, 4: 5, 5: 7, 6: 7},
+    6: {0: 1, 1: 6, 2: 3, 3: 6, 4: 5, 5: 6},
     5: {0: 1, 1: 5, 2: 3, 3: 5, 4: 5},
     4: {0: 1, 1: 4, 2: 3, 3: 4},
     3: {0: 1, 1: 3, 2: 3},
@@ -95,7 +96,7 @@
 
 def kernel(
     ev, eig_in, bmap_in, mom_in, field_out, mom_out,
-    buf, part, other, held, wide, narrow, phase, lanes, plane, line, both, eig, bmap, mom,
+    buf, sums, part, other, held, wide, narrow, phase, lanes, share, own, line, plane, both, eig, bmap, mom,
     load_sem, core_send, core_recv, tree_send, tree_recv, mom_send, mom_recv, greet,
 ):
     site, mode = lax.axis_index("site"), lax.axis_index("mode")
@@ -129,12 +130,15 @@
     expected = jnp.int32(1 + len(near))
     for r in range(ROOTS):
         apart = lax.rem(height - r + 16, 16)
-        expected = expected + jnp.where((apart > 2) & (apart < 14), 1, 0)
+        expected = expected + jnp.where((apart > 2) & (apart < 14), 2, jnp.where(apart == 0, 0, 1))
 
     @pl.when(root)
     def _():
         for step in range(3, 14):
             signal(barrier, at_z(step))
+        for step in range(1, 16):
+            z = lax.rem(height + step, 16)
+            signal(barrier, (z // LINE * 16 + xy, z % LINE * 2 + 1 - core))
         for step in range(1, 16):
             signal(barrier, at_plane(lax.rem(xy + step, 16)))
 
@@ -178,67 +182,79 @@
         for q in range(8):
             part[par, q, 104:112] = jnp.zeros((8, 128), F32)
 
-    def density(early, rows, load):
-        pairs = ((0, 3), (1, 2)) if early else ((0, 1), (2, 3), (0, 2), (1, 3))
-        names = [("d", s, s) for s in range(4)] if early else []
-        names += [(kind, s, r) for s, r in pairs for kind in ("a", "b")]
+    def density(modes, load):
         total = {}
-        for m in range(4):
-            weight = jnp.broadcast_to(weights[m][0:1], (rows, 128))
+        for m in modes:
             inside = {}
             for c in range(3):
                 real = [load(m * 24 + s * 3 + c) for s in range(4)]
                 imag = [load(m * 24 + 12 + s * 3 + c) for s in range(4)]
-                for kind, s, r in names:
+                for key in NAMES:
+                    kind, s, r = key
                     if kind == "b":
                         value = real[s] * imag[r] - imag[s] * real[r]
                     else:
                         value = real[s] * real[r] + imag[s] * imag[r]
-                    key = (kind, s, r)
                     inside[key] = inside[key] + value if c else value
-            for key in names:
-                value = weight * inside[key]
-                total[key] = total[key] + value if m else value
-        out = []
-        for q in range(EARLY) if early else range(EARLY, 8):
-            for par in range(2):
-                terms = TRACES[2 * ORDER[q] + par][1]
-                value = None
-                for positive, _, name in terms:
-                    if value is None:
-                        value = total[name] if positive else -total[name]
-                    else:
-                        value = value + total[name] if positive else value - total[name]
-                if terms[0][1]:
-                    value = value + value
-                out.append((par, q, value))
-        return out
-
-    def groups(early, first, last):
+            for key in NAMES:
+                value = weights[m][0 : inside[key].shape[0]] * inside[key]
+                total[key] = total[key] + value if m != modes[0] else value
+        return total
+
+    def halves(base, size):
+        for first in range(0, size, 8):
+            last = min(first + 8, size)
+            yield first, last - first, lambda p, i=first, j=last: buf[p, pl.ds(base, size)].astype(F32)[i:j]
+
+    def begin(base, size):
+        for first, count, load in halves(base, size):
+            total = density((0, 1), load)
+            for i, key in enumerate(NAMES):
+                sums[i, pl.ds(base + first, count)] = total[key]
+
+    def finish(base, size):
+        for first, count, load in halves(base, size):
+            total = density((2, 3), load)
+            for i, key in enumerate(NAMES):
+                total[key] = total[key] + sums[i, pl.ds(base + first, count)]
+            for q in range(8):
+                for par in range(2):
+                    terms = TRACES[2 * ORDER[q] + par][1]
+                    value = None
+                    for positive, _, name in terms:
+                        if value is None:
+                            value = total[name] if positive else -total[name]
+                        else:
+                            value = value + total[name] if positive else value - total[name]
+                    if terms[0][1]:
+                        value = value + value
+                    part[par, q, pl.ds(base + first, count)] = value
+        rows = pl.ds(base, 16)
+        field = jnp.concatenate([part[par, q, rows] for par in range(2) for q in range(8)], axis=0)
+        high = field.astype(jnp.bfloat16)
+        low = (field - high.astype(F32)).astype(jnp.bfloat16)
+        value = jnp.dot(jnp.concatenate([high, low], axis=1), doubled, preferred_element_type=F32)
+        value = value + jnp.dot(high, rest, preferred_element_type=F32)
+        value = (value.reshape(16, 2, 8, 128) * phase[rows].reshape(1, 2, 8, 128)).sum(axis=1)
+        share[...] += value
+
+    def groups(what, first, last):
         def body(g, carry):
-            base = pl.multiple_of(g * 16, 16)
-            for par, q, value in density(early, 16, lambda p: buf[p, pl.ds(base, 16)].astype(F32)):
-                part[par, q, pl.ds(base, 16)] = value
+            what(pl.multiple_of(g * 16, 16), 16)
             return carry
         lax.fori_loop(first, last, body, 0)
 
-    def tail(early):
-        for par, q, value in density(early, 12, lambda p: buf[p, 96:108].astype(F32)):
-            part[par, q, 96:108] = value
-
-    def to_twin(stage, cut):
+    def to_twin(cut):
         start, size = CUTS[cut]
         return pltpu.make_async_remote_copy(
-            src_ref=part.at[1 - core, pl.ds(4 * stage, 4), pl.ds(start, size)],
-            dst_ref=other.at[pl.ds(4 * stage, 4), pl.ds(start, size)],
-            send_sem=core_send.at[stage, cut], recv_sem=core_recv.at[stage, cut],
-            device_id=twin, device_id_type=MESH,
+            src_ref=part.at[1 - core, :, pl.ds(start, size)], dst_ref=other.at[:, pl.ds(start, size)],
+            send_sem=core_send.at[cut], recv_sem=core_recv.at[cut], device_id=twin, device_id_type=MESH,
         )
 
-    def from_twin(stage, cut):
-        to_twin(stage, cut).wait_recv()
+    def from_twin(cut):
+        to_twin(cut).wait_recv()
         start, size = CUTS[cut]
-        for q in range(4 * stage, 4 * stage + 4):
+        for q in range(8):
             part[core, q, start : start + size] += other[q, start : start + size]
 
     ways = (place, LINE - 1 - place)
@@ -278,15 +294,15 @@
         return [(n, pick(here, [int(k < owner and len(children(owner, k)) > n) for k in range(LINE)]) == 1)
                 for n in range(max(len(children(owner, k)) for k in range(owner)))]
 
-    def send_leaves(owner, cut):
-        for way in range(2):
+    def send_leaves(owner, cut, ways_too=(1, 0)):
+        for way in ways_too:
             @pl.when(leaves(way, owner))
             def _():
                 step_to(way, owner, cut, part.at[core, owner_at(way, owner)]).start()
 
     def send_collected(owner, cut):
         start, size = CUTS[cut]
-        for way in range(2):
+        for way in (1, 0):
             slots = collectors(way, owner)
             if not slots:
                 continue
@@ -308,23 +324,9 @@
     rest = narrow[...].astype(jnp.bfloat16)
     doubled = jnp.concatenate([top, top], axis=0)
 
-    def project(stage):
-        share = part[core, 4 * stage : 4 * stage + 4].reshape(4 * PAD, 128)
-        high = share.astype(jnp.bfloat16)
-        low = (share - high.astype(F32)).astype(jnp.bfloat16)
-        value = jnp.dot(jnp.concatenate([high, low], axis=1), doubled, preferred_element_type=F32)
-        value = value + jnp.dot(high, rest, preferred_element_type=F32)
-        value = (value.reshape(4, PAD, 128) * phase[...][None]).reshape(4, 14, 8, 128).sum(axis=1)
-        folded = []
-        for q in range(4):
-            one = value[q] + pltpu.roll(value[q], 4, 0)
-            folded.append(one + pltpu.roll(one, 64, 1))
-        pairs = [jnp.where(upper, folded[2 * j], folded[2 * j + 1]) for j in range(2)]
-        line[height, 8 * stage : 8 * stage + 8] = jnp.where(lane < 64, pairs[0], pairs[1])
-
-    def passed(buffer, slot, stage, device):
+    def passed(source, target, stage, device):
         return pltpu.make_async_remote_copy(
-            src_ref=buffer.at[slot], dst_ref=buffer.at[slot], send_sem=mom_send.at[stage], recv_sem=mom_recv.at[stage],
+            src_ref=source, dst_ref=target, send_sem=mom_send.at[stage], recv_sem=mom_recv.at[stage],
             device_id=device, device_id_type=MESH,
         )
 
@@ -335,76 +337,96 @@
             device_id=twin, device_id_type=MESH,
         )
 
-    for copy in loads:
+    share[...] = jnp.zeros_like(share)
+    for copy in loads[:2]:
         copy.wait()
-    groups(True, 0, 4)
+    groups(begin, 0, 6)
+    begin(96, 12)
+    for copy in loads[2:]:
+        copy.wait()
     pl.semaphore_wait(barrier, expected)
     for i, step in enumerate((2, -2)):
         signal(greet.at[i], at_z(step))
-    to_twin(0, 0).start()
-    groups(True, 4, 6)
-    tail(True)
-    to_twin(0, 1).start()
-    groups(False, 0, 4)
-    to_twin(1, 0).start()
-    for cut in range(2):
-        from_twin(0, cut)
-        for owner in (7, 6):
-            send_leaves(owner, cut)
-    groups(False, 4, 6)
-    tail(False)
-    to_twin(1, 1).start()
-    project(0)
-    for cut in range(2):
-        from_twin(1, cut)
-    project(1)
+    groups(finish, 0, 4)
+    to_twin(0).start()
+    groups(finish, 4, 6)
+    finish(96, 12)
+    to_twin(1).start()
+
+    slot = 2 * height + core
+    for par in range(2):
+        for i in range(2):
+            folded = []
+            for q in range(4):
+                one = share[8 * par + 4 * i + q]
+                one = one + pltpu.roll(one, 4, 0)
+                folded.append(one + pltpu.roll(one, 64, 1))
+            pairs = [jnp.where(upper, folded[2 * j], folded[2 * j + 1]) for j in range(2)]
+            own[par, 8 * i : 8 * i + 8] = jnp.where(lane < 64, pairs[0], pairs[1])
+
+    def to_root(r, par):
+        return passed(own.at[par], line.at[slot], 0, (xy, 2 * r + par))
+
     for r in range(ROOTS):
         @pl.when(height != r)
         def _():
-            passed(line, height, 0, (xy, 2 * r + core)).start()
+            for par in range(2):
+                to_root(r, par).start()
+
+    @pl.when(root)
+    def _():
+        passed(own.at[1 - core], line.at[slot], 0, twin).start()
+        line[slot] = own[core]
+
+    for cut in range(2):
+        from_twin(cut)
+        for owner in (7, 6):
+            send_leaves(owner, cut)
     for owner in (5, 4, 3, 2, 1):
         for cut in range(2):
-            send_leaves(owner, cut)
+            send_leaves(owner, cut, (0,))
 
     for i in range(2):
         pl.semaphore_wait(greet.at[i], 1)
-    for i, step in enumerate((1, -1)):
+    for i, step in enumerate((2, -2)):
         signal(greet.at[2 + i], at_z(step))
-    for owner in (7, 6, 5, 4, 3, 2):
+    for i in range(2):
+        pl.semaphore_wait(greet.at[2 + i], 1)
+    for owner in (7, 6):
         for cut in range(2):
-            if owner == 7 and cut == 0:
-                for i in range(2):
-                    pl.semaphore_wait(greet.at[2 + i], 1)
             send_collected(owner, cut)
-
-    def added(buffer):
-        value = buffer[0]
-        for i in range(1, 16):
-            value = value + buffer[i]
+    mine = pick(place, [ORDER.index(p) for p in range(LINE)])
+
+    def take(way, owner, slots):
+        for cut, (start, size) in enumerate(CUTS):
+            for n in slots:
+                arrived(way, owner, n, cut)
+                part[core, mine, start : start + size] += held[way, owner, n, start : start + size]
+
+    for way in range(2):
+        @pl.when(ways[way] == 7)
+        def _():
+            take(way, 7, (3,))
+    for owner in (5, 4, 3, 2, 1):
+        for cut in range(2):
+            send_leaves(owner, cut, (1,))
+
+    def added(buffer, first, count):
+        value = buffer[first]
+        for i in range(1, count):
+            value = value + buffer[first + i]
         return value
 
     @pl.when(root)
     def _():
-        whole(line, 15, 0).wait_recv()
-        plane[xy] = added(line)
+        whole(line, 31, 0).wait_recv()
+        plane[xy] = added(line, 0, 32)
         for step in range(1, 16):
-            passed(plane, xy, 1, at_plane(lax.rem(xy + step, 16))).start()
-
-    mine = pick(place, [ORDER.index(p) for p in range(LINE)])
-    for cut, (start, size) in enumerate(CUTS):
-        rows = pl.ds(start, size)
-        for way in range(2):
-            for owner in range(1, LINE):
-                count = len(children(owner, owner))
-                @pl.when(ways[way] == owner)
-                def _():
-                    for n in range(count):
-                        arrived(way, owner, n, cut)
-                        part[core, mine, rows] += held[way, owner, n, start : start + size]
-    total = part[core, mine]
-    imaginary = pick(mode, [int(t[0]) for t in TRACES]) == 1
-    field_out[0:ROWS] = jnp.where(imaginary, 0.0, total)[0:ROWS]
-    field_out[ROWS : 2 * ROWS] = jnp.where(imaginary, total, 0.0)[0:ROWS]
+            passed(plane.at[xy], plane.at[xy], 1, at_plane(lax.rem(xy + step, 16))).start()
+
+    for owner in (5, 4, 3, 2):
+        for cut in range(2):
+            send_collected(owner, cut)
 
     def spread_out(start):
         for r in range(ROOTS):
@@ -412,16 +434,29 @@
             def _():
                 for z in (8, 9, 10, 11, 12, 13, 14, 15) if r == 0 else (7, 6, 5, 4, 3, 2):
                     for c in range(2):
-                        copy = passed(both, core, 2, (z // LINE * 16 + xy, z % LINE * 2 + c))
+                        copy = passed(both.at[core], both.at[core], 2, (z // LINE * 16 + xy, z % LINE * 2 + c))
                         copy.start() if start else copy.wait_send()
 
     @pl.when(root)
     def _():
         whole(plane, 15, 1).wait_recv()
-        both[core] = added(plane) * (L**-1.5)
-        passed(both, core, 2, twin).start()
+        both[core] = added(plane, 0, 16) * (L**-1.5)
+        passed(both.at[core], both.at[core], 2, twin).start()
         spread_out(True)
-        passed(both, core, 2, twin).wait_recv()
+
+    for way in range(2):
+        for owner in range(1, LINE):
+            @pl.when(ways[way] == owner)
+            def _():
+                take(way, owner, range(3 if owner == 7 else len(children(owner, owner))))
+    total = part[core, mine]
+    imaginary = pick(mode, [int(t[0]) for t in TRACES]) == 1
+    field_out[0:ROWS] = jnp.where(imaginary, 0.0, total)[0:ROWS]
+    field_out[ROWS : 2 * ROWS] = jnp.where(imaginary, total, 0.0)[0:ROWS]
+
+    @pl.when(root)
+    def _():
+        passed(both.at[core], both.at[core], 2, twin).wait_recv()
 
     @pl.when(jnp.logical_not(root))
     def _():
@@ -437,13 +472,13 @@
             mom_out[0, n] = s if TRACES[n][0] else c
             mom_out[1, n] = c if TRACES[n][0] else -s
 
-    for stage in range(2):
-        for cut in range(2):
-            to_twin(stage, cut).wait_send()
+    for cut in range(2):
+        to_twin(cut).wait_send()
     for r in range(ROOTS):
         @pl.when(height != r)
         def _():
-            passed(line, height, 0, twin).wait_send()
+            for par in range(2):
+                to_root(r, par).wait_send()
     for way in range(2):
         for owner in range(1, LINE):
             @pl.when(ways[way] < owner)
@@ -456,8 +491,9 @@
 
     @pl.when(root)
     def _():
+        passed(own.at[1 - core], line.at[slot], 0, twin).wait_send()
         whole(plane, 15, 1).wait_send()
-        passed(both, core, 2, twin).wait_send()
+        passed(both.at[core], both.at[core], 2, twin).wait_send()
         spread_out(False)
 
 
@@ -488,6 +524,7 @@
         out_specs=(pl.BlockSpec(memory_space=pltpu.VMEM), pl.BlockSpec(memory_space=pltpu.VMEM)),
         scratch_shapes=[
             vmem((96, ROWS, 128), jnp.bfloat16),
+            vmem((16, PAD, 128), F32),
             vmem((2, 8, PAD, 128), F32),
             vmem((8, PAD, 128), F32),
             vmem((2, LINE, SLOTS, PAD, 128), F32),
@@ -495,15 +532,17 @@
             vmem((128, 128), F32),
             vmem((PAD, 128), F32),
             vmem((8, 128), jnp.int32),
-            vmem((16, 16, 128), F32),
+            vmem((16, 8, 128), F32),
+            vmem((2, 16, 128), F32),
+            vmem((32, 16, 128), F32),
             vmem((16, 16, 128), F32),
             vmem((2, 16, 128), F32),
             pltpu.SMEM((4,), F32),
             pltpu.SMEM((27,), jnp.int32),
             vmem((3, 27), jnp.int32),
             dma((7,)),
-            dma((2, 2)),
-            dma((2, 2)),
+            dma((2,)),
+            dma((2,)),
             dma((2, LINE)),
             dma((2, LINE, SLOTS, 2)),
             dma((3,)),

time: 37.1 us -> 34.1 us (0.919)
  Pallas kernels: 36.3 us -> 33 us
    pallas_call x1, Pallas kernels: 35.6 us -> 32.3 us  [shards(): pl.pallas_call(body, out_shape=tuple((pltpu.VMEM(shape, F32) for shape in...]
where the time goes in v4:
time: 34.1 us; the launch traced here: 33.6 us
  Pallas kernels  33 us (97%)
  between operations  0.64 us (2%)
    pallas_call x1, Pallas kernels, shards(): pl.pallas_call(body, out_shape=tuple((pltpu.VMEM(shape, F32) for shape in...  32.3 us
    pallas_call x1, Pallas kernels, shards(): pl.pallas_call(deliver, out_shape=tuple((jax.ShapeDtypeStruct(shape, F32)...  0.69 us

profile of v4, /device:TPU:1, one launch (start us, length us, event | category | flops | bytes accessed | tf_op | source)
XLA Modules:
  0.0 33.6 jit_solution(3536485983067342215)
XLA Ops:
  0.6 32.3 %loops.1 = (f32[216,128]{1,0:T(8,128)S(1)}, f32[2,16,4,27]{3,2,1,0:T(4,128)S(1)}) custom-call(bf16[4,2,4,3,27,4,128]{6,5,4,3,2,1,0:T(4,128)(2,1)} %bitcast.7, f32[4]{0:T(128)} %refs_0_.1, s32[27]{0:T(128)} %refs_1_.1, s32[3,27]{1,0:T(4,128)} %bitcast.8), custom_call_target="tpu_custom_call" | custom-call | tf_op jit(solution)/shard_map/loops/pallas_call | solution.py:520
  32.9 0.7 %deliver.1 = (f32[216,128]{1,0:T(8,128)}, f32[2,16,4,27]{3,2,1,0:T(4,128)}) custom-call(f32[216,128]{1,0:T(8,128)S(1)} %get-tuple-element.6.field_in, f32[2,16,4,27]{3,2,1,0:T(4,128)S(1)} %get-tuple-element.7.mom_in), custom_call_target="tpu_custom_call" | custom-call | tf_op jit(solution)/shard_map/deliver/pallas_call | solution.py:555

commit v5 on v4

--- a/solution.py
+++ b/solution.py
@@ -96,7 +96,7 @@
 
 def kernel(
     ev, eig_in, bmap_in, mom_in, field_out, mom_out,
-    buf, sums, part, other, held, wide, narrow, phase, lanes, share, own, line, plane, both, eig, bmap, mom,
+    buf, sums, part, other, held, wide, narrow, phase, lanes, own, line, plane, both, eig, bmap, mom,
     load_sem, core_send, core_recv, tree_send, tree_recv, mom_send, mom_recv, greet,
 ):
     site, mode = lax.axis_index("site"), lax.axis_index("mode")
@@ -115,13 +115,16 @@
         pl.semaphore_signal(sem, inc=1, device_id=device, device_id_type=MESH)
 
     twin = (site, place * 2 + 1 - core)
-    barrier = pltpu.get_barrier_semaphore()
+    loads = [
+        pltpu.make_async_copy(ev.at[pl.ds(48 * m, 48)], buf.at[pl.ds(48 * m, 48)], load_sem.at[m]) for m in range(2)
+    ]
     small = [
-        pltpu.make_async_copy(source, target, load_sem.at[4 + i])
+        pltpu.make_async_copy(source, target, load_sem.at[2 + i])
         for i, (source, target) in enumerate(((eig_in, eig), (bmap_in, bmap), (mom_in, mom)))
     ]
-    for copy in small:
+    for copy in small + loads:
         copy.start()
+    barrier = pltpu.get_barrier_semaphore()
     near = (1, -1, 2, -2)
     root = height < ROOTS
     signal(barrier, twin)
@@ -143,12 +146,6 @@
             signal(barrier, at_plane(lax.rem(xy + step, 16)))
 
     expected = expected + jnp.where(root, 15, 0)
-
-    loads = [
-        pltpu.make_async_copy(ev.at[pl.ds(24 * m, 24)], buf.at[pl.ds(24 * m, 24)], load_sem.at[m]) for m in range(4)
-    ]
-    for copy in loads:
-        copy.start()
 
     for copy in small:
         copy.wait()
@@ -229,14 +226,16 @@
                     if terms[0][1]:
                         value = value + value
                     part[par, q, pl.ds(base + first, count)] = value
-        rows = pl.ds(base, 16)
+
+    def project(start, size):
+        rows = pl.ds(start, size)
         field = jnp.concatenate([part[par, q, rows] for par in range(2) for q in range(8)], axis=0)
         high = field.astype(jnp.bfloat16)
         low = (field - high.astype(F32)).astype(jnp.bfloat16)
-        value = jnp.dot(jnp.concatenate([high, low], axis=1), doubled, preferred_element_type=F32)
-        value = value + jnp.dot(high, rest, preferred_element_type=F32)
-        value = (value.reshape(16, 2, 8, 128) * phase[rows].reshape(1, 2, 8, 128)).sum(axis=1)
-        share[...] += value
+        value = jnp.dot(jnp.concatenate([high, low], axis=1), tables, preferred_element_type=F32)
+        value = value[:, 0:128] + value[:, 128:256]
+        value = (value.reshape(16, size // 8, 8, 128) * phase[rows].reshape(1, size // 8, 8, 128)).sum(axis=1)
+        return value
 
     def groups(what, first, last):
         def body(g, carry):
@@ -259,70 +258,58 @@
 
     ways = (place, LINE - 1 - place)
 
-    def owner_at(way, owner):
-        return ORDER.index(owner if way == 0 else LINE - 1 - owner)
-
-    def step_to(way, owner, cut, source):
-        here = ways[way]
-        parents = [TREE[owner].get(k, owner) for k in range(LINE)]
-        slots = [children(owner, TREE[owner][k]).index(k) if k in TREE[owner] else 0 for k in range(LINE)]
-        to = pick(here, parents)
-        target = to if way == 0 else LINE - 1 - to
-        start, size = CUTS[cut]
-        slot = pick(here, slots)
+    def chip(way, k):
+        return k if way == 0 else LINE - 1 - k
+
+    def routes(way, owner):
+        here, tree = ways[way], TREE[owner]
+        sends = [k in tree for k in range(LINE)]
+        straight = [sends[k] and tree[k] == owner for k in range(LINE)]
+        to = pick(here, [chip(way, tree[k]) if sends[k] else 0 for k in range(LINE)])
+        box = pick(here, [
+            LINE + SLOTS * way + children(owner, owner).index(k) if straight[k] else chip(way, owner) for k in range(LINE)
+        ])
+        alone = pick(here, [int(sends[k] and not children(owner, k)) for k in range(LINE)]) == 1
+        adds = pick(here, [int(sends[k] and len(children(owner, k)) == 1) for k in range(LINE)]) == 1
+        return to, box, alone, adds
+
+    routed = {(way, owner): routes(way, owner) for way in range(2) for owner in range(1, LINE)}
+
+    def step_to(way, owner):
+        to, box, _, _ = routed[way, owner]
         return pltpu.make_async_remote_copy(
-            src_ref=source.at[pl.ds(start, size)],
-            dst_ref=held.at[way, owner, slot, pl.ds(start, size)],
-            send_sem=tree_send.at[way, owner], recv_sem=tree_recv.at[way, owner, slot, cut],
-            device_id=(site, target * 2 + core), device_id_type=MESH,
+            src_ref=part.at[core, ORDER.index(chip(way, owner))], dst_ref=held.at[box],
+            send_sem=tree_send.at[chip(way, owner)], recv_sem=tree_recv.at[box],
+            device_id=(site, to * 2 + core), device_id_type=MESH,
         )
 
-    def arrived(way, owner, slot, cut):
-        start, size = CUTS[cut]
-        ref = held.at[way, owner, slot, pl.ds(start, size)]
+    def arrived(box):
+        ref = held.at[box]
         pltpu.make_async_remote_copy(
-            src_ref=ref, dst_ref=ref, send_sem=tree_send.at[way, owner], recv_sem=tree_recv.at[way, owner, slot, cut],
+            src_ref=ref, dst_ref=ref, send_sem=tree_send.at[0], recv_sem=tree_recv.at[box],
             device_id=twin, device_id_type=MESH,
         ).wait_recv()
 
-    def leaves(way, owner):
-        here = ways[way]
-        return pick(here, [int(k < owner and not children(owner, k)) for k in range(LINE)]) == 1
-
-    def collectors(way, owner):
-        here = ways[way]
-        return [(n, pick(here, [int(k < owner and len(children(owner, k)) > n) for k in range(LINE)]) == 1)
-                for n in range(max(len(children(owner, k)) for k in range(owner)))]
-
-    def send_leaves(owner, cut, ways_too=(1, 0)):
+    def send_leaves(owner, ways_too=(1, 0)):
         for way in ways_too:
-            @pl.when(leaves(way, owner))
+            @pl.when(routed[way, owner][2])
             def _():
-                step_to(way, owner, cut, part.at[core, owner_at(way, owner)]).start()
-
-    def send_collected(owner, cut):
-        start, size = CUTS[cut]
+                step_to(way, owner).start()
+
+    def send_collected(owner):
         for way in (1, 0):
-            slots = collectors(way, owner)
-            if not slots:
-                continue
-
-            @pl.when(slots[0][1])
+            @pl.when(routed[way, owner][3])
             def _():
-                for n, here in slots:
-                    if n == 0:
-                        arrived(way, owner, 0, cut)
-                        held[way, owner, 0, start : start + size] += part[core, owner_at(way, owner), start : start + size]
-                    else:
-                        @pl.when(here)
-                        def _():
-                            arrived(way, owner, n, cut)
-                            held[way, owner, 0, start : start + size] += held[way, owner, n, start : start + size]
-                step_to(way, owner, cut, held.at[way, owner, 0]).start()
+                box = chip(way, owner)
+                arrived(box)
+                part[core, ORDER.index(box)] += held[box]
+                step_to(way, owner).start()
 
     top = wide[...].astype(jnp.bfloat16)
     rest = narrow[...].astype(jnp.bfloat16)
-    doubled = jnp.concatenate([top, top], axis=0)
+    tables = jnp.concatenate(
+        [jnp.concatenate([top, rest], axis=1), jnp.concatenate([top, jnp.zeros_like(rest)], axis=1)], axis=0
+    )
 
     def passed(source, target, stage, device):
         return pltpu.make_async_remote_copy(
@@ -337,21 +324,21 @@
             device_id=twin, device_id_type=MESH,
         )
 
-    share[...] = jnp.zeros_like(share)
-    for copy in loads[:2]:
-        copy.wait()
+    loads[0].wait()
     groups(begin, 0, 6)
     begin(96, 12)
-    for copy in loads[2:]:
-        copy.wait()
+    loads[1].wait()
+    groups(finish, 0, 4)
     pl.semaphore_wait(barrier, expected)
+    to_twin(0).start()
     for i, step in enumerate((2, -2)):
         signal(greet.at[i], at_z(step))
-    groups(finish, 0, 4)
-    to_twin(0).start()
-    groups(finish, 4, 6)
+    share = project(*CUTS[0])
+    finish(64, 16)
+    finish(80, 16)
     finish(96, 12)
     to_twin(1).start()
+    share = share + project(*CUTS[1])
 
     slot = 2 * height + core
     for par in range(2):
@@ -380,11 +367,10 @@
 
     for cut in range(2):
         from_twin(cut)
-        for owner in (7, 6):
-            send_leaves(owner, cut)
+    for owner in (7, 6):
+        send_leaves(owner)
     for owner in (5, 4, 3, 2, 1):
-        for cut in range(2):
-            send_leaves(owner, cut, (0,))
+        send_leaves(owner, (0,))
 
     for i in range(2):
         pl.semaphore_wait(greet.at[i], 1)
@@ -393,23 +379,20 @@
     for i in range(2):
         pl.semaphore_wait(greet.at[2 + i], 1)
     for owner in (7, 6):
-        for cut in range(2):
-            send_collected(owner, cut)
+        send_collected(owner)
     mine = pick(place, [ORDER.index(p) for p in range(LINE)])
 
-    def take(way, owner, slots):
-        for cut, (start, size) in enumerate(CUTS):
-            for n in slots:
-                arrived(way, owner, n, cut)
-                part[core, mine, start : start + size] += held[way, owner, n, start : start + size]
+    def take(way, n):
+        box = LINE + SLOTS * way + n
+        arrived(box)
+        part[core, mine] += held[box]
 
     for way in range(2):
-        @pl.when(ways[way] == 7)
+        @pl.when(ways[way] == LINE - 1)
         def _():
-            take(way, 7, (3,))
+            take(way, SLOTS - 1)
     for owner in (5, 4, 3, 2, 1):
-        for cut in range(2):
-            send_leaves(owner, cut, (1,))
+        send_leaves(owner, (1,))
 
     def added(buffer, first, count):
         value = buffer[first]
@@ -425,8 +408,7 @@
             passed(plane.at[xy], plane.at[xy], 1, at_plane(lax.rem(xy + step, 16))).start()
 
     for owner in (5, 4, 3, 2):
-        for cut in range(2):
-            send_collected(owner, cut)
+        send_collected(owner)
 
     def spread_out(start):
         for r in range(ROOTS):
@@ -445,10 +427,13 @@
         spread_out(True)
 
     for way in range(2):
-        for owner in range(1, LINE):
-            @pl.when(ways[way] == owner)
+        counts = [0] + [len(children(owner, owner)) for owner in range(1, LINE)]
+        counts[LINE - 1] = SLOTS - 1
+        count = pick(ways[way], counts)
+        for n in range(SLOTS - 1):
+            @pl.when(count > n)
             def _():
-                take(way, owner, range(3 if owner == 7 else len(children(owner, owner))))
+                take(way, n)
     total = part[core, mine]
     imaginary = pick(mode, [int(t[0]) for t in TRACES]) == 1
     field_out[0:ROWS] = jnp.where(imaginary, 0.0, total)[0:ROWS]
@@ -479,15 +464,14 @@
         def _():
             for par in range(2):
                 to_root(r, par).wait_send()
-    for way in range(2):
-        for owner in range(1, LINE):
-            @pl.when(ways[way] < owner)
-            def _():
-                ref = held.at[way, owner, 0]
-                pltpu.make_async_remote_copy(
-                    src_ref=ref, dst_ref=ref, send_sem=tree_send.at[way, owner], recv_sem=tree_recv.at[way, owner, 0, 0],
-                    device_id=twin, device_id_type=MESH,
-                ).wait_send()
+    for d in range(LINE):
+        @pl.when(place != d)
+        def _():
+            ref = held.at[0]
+            pltpu.make_async_remote_copy(
+                src_ref=ref, dst_ref=ref, send_sem=tree_send.at[d], recv_sem=tree_recv.at[0],
+                device_id=twin, device_id_type=MESH,
+            ).wait_send()
 
     @pl.when(root)
     def _():
@@ -527,12 +511,11 @@
             vmem((16, PAD, 128), F32),
             vmem((2, 8, PAD, 128), F32),
             vmem((8, PAD, 128), F32),
-            vmem((2, LINE, SLOTS, PAD, 128), F32),
+            vmem((LINE + 2 * SLOTS, PAD, 128), F32),
             vmem((128, 128), F32),
             vmem((128, 128), F32),
             vmem((PAD, 128), F32),
             vmem((8, 128), jnp.int32),
-            vmem((16, 8, 128), F32),
             vmem((2, 16, 128), F32),
             vmem((32, 16, 128), F32),
             vmem((16, 16, 128), F32),
@@ -540,11 +523,11 @@
             pltpu.SMEM((4,), F32),
             pltpu.SMEM((27,), jnp.int32),
             vmem((3, 27), jnp.int32),
-            dma((7,)),
+            dma((5,)),
             dma((2,)),
             dma((2,)),
-            dma((2, LINE)),
-            dma((2, LINE, SLOTS, 2)),
+            dma((LINE,)),
+            dma((LINE + 2 * SLOTS,)),
             dma((3,)),
             dma((3,)),
             pltpu.SemaphoreType.REGULAR((4,)),

time: 34.1 us -> 31.9 us (0.935)
  Pallas kernels: 33 us -> 30.9 us
    pallas_call x1, Pallas kernels: 32.3 us -> 30.2 us  [shards(): pl.pallas_call(body, out_shape=tuple((pltpu.VMEM(shape, F32) for shape in...]
where the time goes in v5:
time: 31.9 us; the launch traced here: 31.6 us
  Pallas kernels  30.9 us (97%)
  between operations  0.64 us (2%)
    pallas_call x1, Pallas kernels, shards(): pl.pallas_call(body, out_shape=tuple((pltpu.VMEM(shape, F32) for shape in...  30.2 us
    pallas_call x1, Pallas kernels, shards(): pl.pallas_call(deliver, out_shape=tuple((jax.ShapeDtypeStruct(shape, F32)...  0.69 us

profile of v5, /device:TPU:1, one launch (start us, length us, event | category | flops | bytes accessed | tf_op | source)
XLA Modules:
  0.0 31.6 jit_solution(1063692065084510503)
XLA Ops:
  0.6 30.2 %loops.1 = (f32[216,128]{1,0:T(8,128)S(1)}, f32[2,16,4,27]{3,2,1,0:T(4,128)S(1)}) custom-call(bf16[4,2,4,3,27,4,128]{6,5,4,3,2,1,0:T(4,128)(2,1)} %bitcast.7, f32[4]{0:T(128)} %refs_0_.1, s32[27]{0:T(128)} %refs_1_.1, s32[3,27]{1,0:T(4,128)} %bitcast.8), custom_call_target="tpu_custom_call" | custom-call | tf_op jit(solution)/shard_map/loops/pallas_call | solution.py:504
  30.9 0.7 %deliver.1 = (f32[216,128]{1,0:T(8,128)}, f32[2,16,4,27]{3,2,1,0:T(4,128)}) custom-call(f32[216,128]{1,0:T(8,128)S(1)} %get-tuple-element.6.field_in, f32[2,16,4,27]{3,2,1,0:T(4,128)S(1)} %get-tuple-element.7.mom_in), custom_call_target="tpu_custom_call" | custom-call | tf_op jit(solution)/shard_map/deliver/pallas_call | solution.py:538

commit v6 on v5

--- a/solution.py
+++ b/solution.py
@@ -30,6 +30,9 @@
     1: {0: 1},
 }
 SLOTS = 4
+FAR_FIRST = sorted(
+    ((dy, dx) for dy in range(4) for dx in range(4) if dy or dx), key=lambda s: -min(s[0], 4 - s[0]) - min(s[1], 4 - s[1])
+)
 
 
 def children(owner, place):
@@ -157,14 +160,13 @@
     along = [jnp.broadcast_to(spread[i : i + 1], (8, 128)) for i in range(3)]
     lane = lax.broadcasted_iota(jnp.int32, (8, 128), 1)
     row = lax.broadcasted_iota(jnp.int32, (8, 128), 0)
-    quarter = jnp.where(lane < 32, 0.0, jnp.where(lane < 64, -12.0, jnp.where(lane < 96, 12.0, 0.0)))
+    quarter = jnp.where(lane % 64 < 32, 0.0, -12.0)
     inner = along[2] * row.astype(F32) + quarter
     for i in range(16):
         values = cosine(inner + along[1] * float(i % 4) + along[0] * float(i // 4))
         top = values.astype(jnp.bfloat16).astype(F32)
-        lanes_f = (values - top)
-        wide[8 * i : 8 * i + 8] = top
-        narrow[8 * i : 8 * i + 8] = lanes_f
+        wide[8 * i : 8 * i + 8] = jnp.where(lane < 64, top, values - top)
+        narrow[8 * i : 8 * i + 8] = jnp.where(lane < 64, top, 0.0)
     turn = jnp.where(lane < 64, 0.0, -12.0)
     upper = row < 4
     for i in range(14):
@@ -233,7 +235,7 @@
         high = field.astype(jnp.bfloat16)
         low = (field - high.astype(F32)).astype(jnp.bfloat16)
         value = jnp.dot(jnp.concatenate([high, low], axis=1), tables, preferred_element_type=F32)
-        value = value[:, 0:128] + value[:, 128:256]
+        value = value + pltpu.roll(value, 64, 1)
         value = (value.reshape(16, size // 8, 8, 128) * phase[rows].reshape(1, size // 8, 8, 128)).sum(axis=1)
         return value
 
@@ -305,11 +307,7 @@
                 part[core, ORDER.index(box)] += held[box]
                 step_to(way, owner).start()
 
-    top = wide[...].astype(jnp.bfloat16)
-    rest = narrow[...].astype(jnp.bfloat16)
-    tables = jnp.concatenate(
-        [jnp.concatenate([top, rest], axis=1), jnp.concatenate([top, jnp.zeros_like(rest)], axis=1)], axis=0
-    )
+    tables = jnp.concatenate([wide[...], narrow[...]], axis=0).astype(jnp.bfloat16)
 
     def passed(source, target, stage, device):
         return pltpu.make_async_remote_copy(
@@ -329,31 +327,27 @@
     begin(96, 12)
     loads[1].wait()
     groups(finish, 0, 4)
-    pl.semaphore_wait(barrier, expected)
-    to_twin(0).start()
-    for i, step in enumerate((2, -2)):
-        signal(greet.at[i], at_z(step))
     share = project(*CUTS[0])
     finish(64, 16)
     finish(80, 16)
     finish(96, 12)
-    to_twin(1).start()
     share = share + project(*CUTS[1])
 
     slot = 2 * height + core
     for par in range(2):
         for i in range(2):
-            folded = []
-            for q in range(4):
-                one = share[8 * par + 4 * i + q]
-                one = one + pltpu.roll(one, 4, 0)
-                folded.append(one + pltpu.roll(one, 64, 1))
+            folded = [share[8 * par + 4 * i + q] for q in range(4)]
+            folded = [one + pltpu.roll(one, 4, 0) for one in folded]
             pairs = [jnp.where(upper, folded[2 * j], folded[2 * j + 1]) for j in range(2)]
-            own[par, 8 * i : 8 * i + 8] = jnp.where(lane < 64, pairs[0], pairs[1])
+            pairs = [one + jnp.where(lane < 32, -pltpu.roll(one, 32, 1), pltpu.roll(one, 96, 1)) for one in pairs]
+            own[par, 8 * i : 8 * i + 8] = jnp.where(lane < 64, pairs[0], pltpu.roll(pairs[1], 64, 1))
 
     def to_root(r, par):
         return passed(own.at[par], line.at[slot], 0, (xy, 2 * r + par))
 
+    pl.semaphore_wait(barrier, expected)
+    for i, step in enumerate((2, -2)):
+        signal(greet.at[i], at_z(step))
     for r in range(ROOTS):
         @pl.when(height != r)
         def _():
@@ -365,6 +359,8 @@
         passed(own.at[1 - core], line.at[slot], 0, twin).start()
         line[slot] = own[core]
 
+    for cut in range(2):
+        to_twin(cut).start()
     for cut in range(2):
         from_twin(cut)
     for owner in (7, 6):
@@ -404,8 +400,9 @@
     def _():
         whole(line, 31, 0).wait_recv()
         plane[xy] = added(line, 0, 32)
-        for step in range(1, 16):
-            passed(plane.at[xy], plane.at[xy], 1, at_plane(lax.rem(xy + step, 16))).start()
+        for dy, dx in FAR_FIRST:
+            column = lax.rem(xy // 4 + dy, 4) * 4 + lax.rem(xy % 4 + dx, 4)
+            passed(plane.at[xy], plane.at[xy], 1, at_plane(column)).start()
 
     for owner in (5, 4, 3, 2):
         send_collected(owner)
@@ -414,7 +411,7 @@
         for r in range(ROOTS):
             @pl.when(height == r)
             def _():
-                for z in (8, 9, 10, 11, 12, 13, 14, 15) if r == 0 else (7, 6, 5, 4, 3, 2):
+                for z in (8, 9, 10, 11, 12, 13, 14, 15) if r == 0 else (2, 3, 4, 5, 6, 7):
                     for c in range(2):
                         copy = passed(both.at[core], both.at[core], 2, (z // LINE * 16 + xy, z % LINE * 2 + c))
                         copy.start() if start else copy.wait_send()

time: 31.9 us -> 31.4 us (0.984)
  no operation moved by 1% of the time
where the time goes in v6:
time: 31.4 us; the launch traced here: 31.3 us
  Pallas kernels  30.6 us (97%)
  between operations  0.64 us (2%)
    pallas_call x1, Pallas kernels, shards(): pl.pallas_call(body, out_shape=tuple((pltpu.VMEM(shape, F32) for shape in...  30 us
    pallas_call x1, Pallas kernels, shards(): pl.pallas_call(deliver, out_shape=tuple((jax.ShapeDtypeStruct(shape, F32)...  0.69 us

profile of v6, /device:TPU:1, one launch (start us, length us, event | category | flops | bytes accessed | tf_op | source)
XLA Modules:
  0.0 31.3 jit_solution(1743786669315147066)
XLA Ops:
  0.6 30.0 %loops.1 = (f32[216,128]{1,0:T(8,128)S(1)}, f32[2,16,4,27]{3,2,1,0:T(4,128)S(1)}) custom-call(bf16[4,2,4,3,27,4,128]{6,5,4,3,2,1,0:T(4,128)(2,1)} %bitcast.7, f32[4]{0:T(128)} %refs_0_.1, s32[27]{0:T(128)} %refs_1_.1, s32[3,27]{1,0:T(4,128)} %bitcast.8), custom_call_target="tpu_custom_call" | custom-call | tf_op jit(solution)/shard_map/loops/pallas_call | solution.py:501
  30.6 0.7 %deliver.1 = (f32[216,128]{1,0:T(8,128)}, f32[2,16,4,27]{3,2,1,0:T(4,128)}) custom-call(f32[216,128]{1,0:T(8,128)S(1)} %get-tuple-element.6.field_in, f32[2,16,4,27]{3,2,1,0:T(4,128)S(1)} %get-tuple-element.7.mom_in), custom_call_target="tpu_custom_call" | custom-call | tf_op jit(solution)/shard_map/deliver/pallas_call | solution.py:535

commit v7 on v6

--- a/solution.py
+++ b/solution.py
@@ -245,18 +245,10 @@
             return carry
         lax.fori_loop(first, last, body, 0)
 
-    def to_twin(cut):
-        start, size = CUTS[cut]
-        return pltpu.make_async_remote_copy(
-            src_ref=part.at[1 - core, :, pl.ds(start, size)], dst_ref=other.at[:, pl.ds(start, size)],
-            send_sem=core_send.at[cut], recv_sem=core_recv.at[cut], device_id=twin, device_id_type=MESH,
-        )
-
-    def from_twin(cut):
-        to_twin(cut).wait_recv()
-        start, size = CUTS[cut]
-        for q in range(8):
-            part[core, q, start : start + size] += other[q, start : start + size]
+    to_twin = pltpu.make_async_remote_copy(
+        src_ref=part.at[1 - core], dst_ref=other, send_sem=core_send.at[0], recv_sem=core_recv.at[0],
+        device_id=twin, device_id_type=MESH,
+    )
 
     ways = (place, LINE - 1 - place)
 
@@ -359,10 +351,10 @@
         passed(own.at[1 - core], line.at[slot], 0, twin).start()
         line[slot] = own[core]
 
-    for cut in range(2):
-        to_twin(cut).start()
-    for cut in range(2):
-        from_twin(cut)
+    to_twin.start()
+    to_twin.wait_recv()
+    for q in range(8):
+        part[core, q] += other[q]
     for owner in (7, 6):
         send_leaves(owner)
     for owner in (5, 4, 3, 2, 1):
@@ -436,15 +428,7 @@
     field_out[0:ROWS] = jnp.where(imaginary, 0.0, total)[0:ROWS]
     field_out[ROWS : 2 * ROWS] = jnp.where(imaginary, total, 0.0)[0:ROWS]
 
-    @pl.when(root)
-    def _():
-        passed(both.at[core], both.at[core], 2, twin).wait_recv()
-
-    @pl.when(jnp.logical_not(root))
-    def _():
-        whole(both, 2, 2).wait_recv()
-
-    for par in range(2):
+    def laid_out(par):
         value = both[par]
         turned = [value] + [pltpu.roll(value, 128 - s, 1) for s in (32, 64, 96)]
         for q in range(8):
@@ -454,8 +438,25 @@
             mom_out[0, n] = s if TRACES[n][0] else c
             mom_out[1, n] = c if TRACES[n][0] else -s
 
-    for cut in range(2):
-        to_twin(cut).wait_send()
+    @pl.when(root)
+    def _():
+        for par in range(2):
+            @pl.when(core == par)
+            def _():
+                laid_out(par)
+        passed(both.at[core], both.at[core], 2, twin).wait_recv()
+        for par in range(2):
+            @pl.when(core != par)
+            def _():
+                laid_out(par)
+
+    @pl.when(jnp.logical_not(root))
+    def _():
+        whole(both, 2, 2).wait_recv()
+        for par in range(2):
+            laid_out(par)
+
+    to_twin.wait_send()
     for r in range(ROOTS):
         @pl.when(height != r)
         def _():
@@ -521,8 +522,8 @@
             pltpu.SMEM((27,), jnp.int32),
             vmem((3, 27), jnp.int32),
             dma((5,)),
-            dma((2,)),
-            dma((2,)),
+            dma((1,)),
+            dma((1,)),
             dma((LINE,)),
             dma((LINE + 2 * SLOTS,)),
             dma((3,)),

time: 31.4 us -> 31.4 us (level)
  no operation moved by 1% of the time
where the time goes in v7:
time: 31.4 us; the launch traced here: 31.3 us
  Pallas kernels  30.6 us (97%)
  between operations  0.64 us (2%)
    pallas_call x1, Pallas kernels, shards(): pl.pallas_call(body, out_shape=tuple((pltpu.VMEM(shape, F32) for shape in...  29.9 us
    pallas_call x1, Pallas kernels, shards(): pl.pallas_call(deliver, out_shape=tuple((jax.ShapeDtypeStruct(shape, F32)...  0.69 us

profile of v7, /device:TPU:1, one launch (start us, length us, event | category | flops | bytes accessed | tf_op | source)
XLA Modules:
  0.0 31.3 jit_solution(17001475208972014216)
XLA Ops:
  0.6 29.9 %loops.1 = (f32[216,128]{1,0:T(8,128)S(1)}, f32[2,16,4,27]{3,2,1,0:T(4,128)S(1)}) custom-call(bf16[4,2,4,3,27,4,128]{6,5,4,3,2,1,0:T(4,128)(2,1)} %bitcast.7, f32[4]{0:T(128)} %refs_0_.1, s32[27]{0:T(128)} %refs_1_.1, s32[3,27]{1,0:T(4,128)} %bitcast.8), custom_call_target="tpu_custom_call" | custom-call | tf_op jit(solution)/shard_map/loops/pallas_call | solution.py:502
  30.6 0.7 %deliver.1 = (f32[216,128]{1,0:T(8,128)}, f32[2,16,4,27]{3,2,1,0:T(4,128)}) custom-call(f32[216,128]{1,0:T(8,128)S(1)} %get-tuple-element.6.field_in, f32[2,16,4,27]{3,2,1,0:T(4,128)S(1)} %get-tuple-element.7.mom_in), custom_call_target="tpu_custom_call" | custom-call | tf_op jit(solution)/shard_map/deliver/pallas_call | solution.py:536
